TPU v7x, 512 devices: a whole 4x4x16 slice. The times are simulated.
512 devices in a mesh: img: 32 (over x_lo, z), blk: 16 (over x_hi, y, core).
Axes of the slice: x: 4 (x_hi: 2, x_lo: 2; x = x_hi * 2 + x_lo), y: 4, z: 16, core: 2. Of those that a mesh axis runs over, the one named last changes fastest.
Arguments:
- images: bfloat16 [32768, 4096], P(('img', 'blk')), may hold values from -16 to 16
- references: bfloat16 [256, 4096], P('blk'), may hold values from -1 to 1
- precision: float32 [32768], P(('img', 'blk')), may hold values from 0.05 to 0.5
- candidates: int32 [32768, 2], P(('img', 'blk')), may hold values from 0 to 255, as said below
Outputs:
- class_average: float32 [256, 4096], P('blk', 'img')
- log_evidence: float32 [32768], P(('img', 'blk'))
Inputs may be any that keep to these rules, and one draw needn't show every extreme that they name: The 2 candidates of an image differ. Classes b * 16 to (b + 1) * 16 - 1 form owner block b. Among the 128 candidate entries of the images of one device, exactly 16 name classes of one owner block, chosen per device, and the other entries are spread over the other owner blocks as evenly as they divide.
All inputs are finite; a program needn't handle non-finite values.
Results may differ from a plain program's by a relative error of at most 0.0028.
Values may be sent and summed in bfloat16 or wider, within the bound.
A program may use at most 64 MiB of HBM per device.

v0:
```python
import math

import jax
import jax.numpy as jnp
from jax import lax
from jax.sharding import PartitionSpec as P

CYCLES = 32
ORDERS = 64
TURNS = 36
PICKS = 2
FEATS = 4096


highest = lax.Precision.HIGHEST


def from_behind(x, axis, by):
    size = lax.axis_size(axis)
    return lax.ppermute(x, axis, [(i, (i + by) % size) for i in range(size)])


def rotation_table():
    orders = jnp.arange(ORDERS, dtype=jnp.int32)
    turn_ids = jnp.arange(TURNS, dtype=jnp.int32)
    phases = turn_ids[:, None] * orders[None, :] % TURNS
    angles = phases.astype(jnp.float32) * (2.0 * math.pi / TURNS)
    return jnp.stack([jnp.cos(angles), -jnp.sin(angles)], axis=2).reshape(TURNS, 2 * ORDERS)


def align(image_rows, posterior, turn_table):
    block_rows = image_rows.shape[0]
    spectrum = jnp.dot(turn_table.T, posterior.reshape(TURNS, -1), precision=highest)
    spectrum = spectrum.reshape(ORDERS, 2, PICKS, block_rows)
    real_part = jnp.transpose(spectrum[:, 0], (2, 1, 0))[..., None]
    imag_part = jnp.transpose(spectrum[:, 1], (2, 1, 0))[..., None]
    pieces = image_rows.reshape(block_rows, ORDERS, 2, CYCLES)
    real_in = pieces[:, None, :, 0, :]
    imag_in = pieces[:, None, :, 1, :]
    real_out = real_in * real_part - imag_in * imag_part
    imag_out = real_in * imag_part + imag_in * real_part
    return jnp.stack([real_out, imag_out], axis=3).reshape(block_rows * PICKS, FEATS)


def block_scores(ref_block, spectra, precision, turn_table):
    ref_count = ref_block.shape[0]
    pieces = ref_block.reshape(ref_count, ORDERS, 2, CYCLES)
    swapped = jnp.stack([-pieces[:, :, 1, :], pieces[:, :, 0, :]], axis=2)
    stacked = jnp.stack([pieces, swapped]).reshape(2, ref_count, ORDERS, 2 * CYCLES)
    squares = jnp.sum(jnp.square(ref_block.astype(jnp.float32)), axis=1)
    harmonic = jnp.einsum("hcmk,imk->mhci", stacked, spectra, preferred_element_type=jnp.float32)
    turned = jnp.dot(turn_table, harmonic.reshape(2 * ORDERS, -1), precision=highest)
    turned = turned.reshape(TURNS, ref_count, -1)
    return precision[None, None, :] * (turned - 0.5 * squares[None, :, None])


def absorb(running, ref_block, owner_id, spectra, precision, pick_rows, turn_table):
    run_peak, run_total, chosen = running
    scores = block_scores(ref_block, spectra, precision, turn_table)
    row_peak = jnp.max(scores, axis=(0, 1))
    new_peak = jnp.maximum(run_peak, row_peak)
    run_total = run_total * jnp.exp(run_peak - new_peak) + jnp.sum(
        jnp.exp(scores - new_peak[None, None, :]), axis=(0, 1)
    )
    local_ids = pick_rows - owner_id * ref_block.shape[0]
    is_pick = (
        local_ids[:, None, :] == jnp.arange(ref_block.shape[0], dtype=jnp.int32)[None, :, None]
    )
    chosen = chosen + jnp.sum(jnp.where(is_pick[None], scores[:, None], 0.0), axis=2)
    return (new_peak, run_total, chosen)


def body(images, references, precision, candidates):
    image_count = images.shape[0]
    blocks = lax.axis_size("blk")
    my_block = lax.axis_index("blk")
    per_owner = references.shape[0]
    classes = blocks * per_owner
    turn_table = rotation_table()
    spectra = images.reshape(image_count, ORDERS, 2 * CYCLES)
    pick_rows = candidates.T

    def take(running, ref_block, owner_id):
        return absorb(running, ref_block, owner_id, spectra, precision, pick_rows, turn_table)

    start = (
        jnp.full((image_count,), -jnp.inf, jnp.float32),
        jnp.zeros((image_count,), jnp.float32),
        jnp.zeros((TURNS, PICKS, image_count), jnp.float32),
    )
    running = take(start, references, my_block)

    def one_turn(turn_index, loop_state):
        ref_block, inner = loop_state
        ref_block = from_behind(ref_block, "blk", 1)
        return (ref_block, take(inner, ref_block, (my_block - turn_index) % blocks))

    ref_block, running = lax.fori_loop(1, blocks, one_turn, (references, running))
    run_peak, run_total, chosen = running
    log_evidence = run_peak + jnp.log(run_total)
    pick_peak = jnp.max(chosen, axis=(0, 1))
    unnorm = jnp.exp(chosen - pick_peak[None, None, :])
    posterior = unnorm / jnp.sum(unnorm, axis=(0, 1))[None, None, :]
    weight_share = jnp.sum(posterior, axis=0)
    contributions = align(images.astype(jnp.float32), posterior, turn_table).astype(jnp.bfloat16)
    flat_picks = candidates.reshape(-1)
    named = flat_picks[None, :] == jnp.arange(classes, dtype=jnp.int32)[:, None]
    local_weight = jnp.sum(jnp.where(named, weight_share.T.reshape(-1)[None, :], 0.0), axis=1)
    class_weight = lax.psum(local_weight, ("img", "blk"))
    pair_count = flat_picks.shape[0]
    slot_count = 2 * pair_count // blocks
    owner_ids = flat_picks // per_owner
    owner_hits = (owner_ids[:, None] == jnp.arange(blocks, dtype=jnp.int32)[None, :]).astype(
        jnp.int32
    )
    position = jnp.sum(jnp.cumsum(owner_hits, axis=0) * owner_hits, axis=1) - 1
    target = owner_ids * slot_count + position
    source_row = (
        jnp.full((blocks * slot_count,), pair_count, jnp.int32)
        .at[target]
        .set(jnp.arange(pair_count, dtype=jnp.int32))
    )
    padded = jnp.concatenate([contributions, jnp.zeros((1, FEATS), jnp.bfloat16)], axis=0)
    labels = jnp.concatenate(
        [(flat_picks % per_owner).astype(jnp.float32), jnp.full((1,), -1.0, jnp.float32)]
    ).astype(jnp.bfloat16)
    send_rows = padded[source_row].reshape(blocks, slot_count, FEATS)
    send_labels = labels[source_row].reshape(blocks, slot_count)
    got_rows, got_labels = (
        lax.all_to_all(send_rows, "blk", split_axis=0, concat_axis=0, tiled=True),
        lax.all_to_all(send_labels, "blk", split_axis=0, concat_axis=0, tiled=True),
    )
    matches = (
        got_labels.reshape(-1)[None, :]
        == jnp.arange(per_owner, dtype=jnp.int32).astype(jnp.bfloat16)[:, None]
    ).astype(jnp.bfloat16)
    partial_sums = jnp.dot(matches, got_rows.reshape(-1, FEATS), preferred_element_type=jnp.float32)
    group_share = lax.psum_scatter(partial_sums, "img", scatter_dimension=1, tiled=True)
    own_weight = lax.dynamic_slice_in_dim(class_weight, my_block * per_owner, per_owner)
    class_average = group_share / (1.0 + own_weight)[:, None]
    return (class_average, log_evidence)


def solution(mesh):
    in_specs = (P(("img", "blk"), None), P("blk", None), P(("img", "blk")), P(("img", "blk"), None))
    out_specs = (P("blk", "img"), P(("img", "blk")))
    return jax.shard_map(body, mesh=mesh, in_specs=in_specs, out_specs=out_specs, check_vma=False)
```

profile of v0, /device:TPU:12, one launch (start us, length us, event | category | flops | bytes accessed | tf_op | source)
XLA Modules:
  0.0 514.3 jit_solution(16147321269480921397)
XLA Ops:
  13.3 9.1 %all-to-all-start = ((bf16[16,1,16]{2,1,0:T(2,128)(2,1)}), bf16[16,1,16]{2,1,0:T(2,128)(2,1)S(1)}, u32[]{:S(2)}, u32[]{:S(2)}) async-start(bf16[16,1,16]{2,1,0:T(2,128)(2,1)} %all_to_all.12), calls=%async_computation | async-start | bytes 16384 | tf_op jit(solution)/shard_map/all_to_all | solution.py:131
  37.0 233.6 %while.21 = (s32[]{:T(128)}, bf16[16,4096]{1,0:T(8,128)(2,1)S(1)}, f32[64]{0:T(128)S(1)}, f32[64]{0:T(128)S(1)}, f32[36,2,64]{2,1,0:T(2,128)S(1)}, /*index=5*/f3...) while((s32[]{:T(128)}, bf16[16,4096]{1,0:T(8,128)(2,1)S(1)}, ...), condition=%wide.region_14.15_spmd, body=%wide.region_7.14_spmd.sunk | while | flops 74504448 | bytes 6860686 | solution.py:98
  39.4 4.1 collective-permute-done
  52.0 4.2 collective-permute-done
  64.7 4.2 collective-permute-done
  77.5 6.9 %collective-permute-done = bf16[16,4096]{1,0:T(8,128)(2,1)S(1)} collective-permute-done((bf16[16,4096]{1,0:T(8,128)(2,1)S(1)}, bf16[16,4096]{1,0:T(8,128)(2,1)S(1)}, u32[]{:S(2)}, u32[]{:S(2)}) %collective-permute-start) | collective-permute-done | bytes 131104 | tf_op jit(solution)/shard_map/while/body/eval_jaxpr/ppermute | solution.py:20
  92.8 7.9 %collective-permute-done = bf16[16,4096]{1,0:T(8,128)(2,1)S(1)} collective-permute-done((bf16[16,4096]{1,0:T(8,128)(2,1)S(1)}, bf16[16,4096]{1,0:T(8,128)(2,1)S(1)}, u32[]{:S(2)}, u32[]{:S(2)}) %collective-permute-start) | collective-permute-done | bytes 131104 | tf_op jit(solution)/shard_map/while/body/eval_jaxpr/ppermute | solution.py:20
  109.2 7.9 %collective-permute-done = bf16[16,4096]{1,0:T(8,128)(2,1)S(1)} collective-permute-done((bf16[16,4096]{1,0:T(8,128)(2,1)S(1)}, bf16[16,4096]{1,0:T(8,128)(2,1)S(1)}, u32[]{:S(2)}, u32[]{:S(2)}) %collective-permute-start) | collective-permute-done | bytes 131104 | tf_op jit(solution)/shard_map/while/body/eval_jaxpr/ppermute | solution.py:20
  125.5 7.9 %collective-permute-done = bf16[16,4096]{1,0:T(8,128)(2,1)S(1)} collective-permute-done((bf16[16,4096]{1,0:T(8,128)(2,1)S(1)}, bf16[16,4096]{1,0:T(8,128)(2,1)S(1)}, u32[]{:S(2)}, u32[]{:S(2)}) %collective-permute-start) | collective-permute-done | bytes 131104 | tf_op jit(solution)/shard_map/while/body/eval_jaxpr/ppermute | solution.py:20
  141.9 7.9 %collective-permute-done = bf16[16,4096]{1,0:T(8,128)(2,1)S(1)} collective-permute-done((bf16[16,4096]{1,0:T(8,128)(2,1)S(1)}, bf16[16,4096]{1,0:T(8,128)(2,1)S(1)}, u32[]{:S(2)}, u32[]{:S(2)}) %collective-permute-start) | collective-permute-done | bytes 131104 | tf_op jit(solution)/shard_map/while/body/eval_jaxpr/ppermute | solution.py:20
  158.2 7.9 %collective-permute-done = bf16[16,4096]{1,0:T(8,128)(2,1)S(1)} collective-permute-done((bf16[16,4096]{1,0:T(8,128)(2,1)S(1)}, bf16[16,4096]{1,0:T(8,128)(2,1)S(1)}, u32[]{:S(2)}, u32[]{:S(2)}) %collective-permute-start) | collective-permute-done | bytes 131104 | tf_op jit(solution)/shard_map/while/body/eval_jaxpr/ppermute | solution.py:20
  174.6 7.9 %collective-permute-done = bf16[16,4096]{1,0:T(8,128)(2,1)S(1)} collective-permute-done((bf16[16,4096]{1,0:T(8,128)(2,1)S(1)}, bf16[16,4096]{1,0:T(8,128)(2,1)S(1)}, u32[]{:S(2)}, u32[]{:S(2)}) %collective-permute-start) | collective-permute-done | bytes 131104 | tf_op jit(solution)/shard_map/while/body/eval_jaxpr/ppermute | solution.py:20
  191.0 7.9 %collective-permute-done = bf16[16,4096]{1,0:T(8,128)(2,1)S(1)} collective-permute-done((bf16[16,4096]{1,0:T(8,128)(2,1)S(1)}, bf16[16,4096]{1,0:T(8,128)(2,1)S(1)}, u32[]{:S(2)}, u32[]{:S(2)}) %collective-permute-start) | collective-permute-done | bytes 131104 | tf_op jit(solution)/shard_map/while/body/eval_jaxpr/ppermute | solution.py:20
  207.3 7.9 %collective-permute-done = bf16[16,4096]{1,0:T(8,128)(2,1)S(1)} collective-permute-done((bf16[16,4096]{1,0:T(8,128)(2,1)S(1)}, bf16[16,4096]{1,0:T(8,128)(2,1)S(1)}, u32[]{:S(2)}, u32[]{:S(2)}) %collective-permute-start) | collective-permute-done | bytes 131104 | tf_op jit(solution)/shard_map/while/body/eval_jaxpr/ppermute | solution.py:20
  223.7 7.9 %collective-permute-done = bf16[16,4096]{1,0:T(8,128)(2,1)S(1)} collective-permute-done((bf16[16,4096]{1,0:T(8,128)(2,1)S(1)}, bf16[16,4096]{1,0:T(8,128)(2,1)S(1)}, u32[]{:S(2)}, u32[]{:S(2)}) %collective-permute-start) | collective-permute-done | bytes 131104 | tf_op jit(solution)/shard_map/while/body/eval_jaxpr/ppermute | solution.py:20
  240.0 7.9 %collective-permute-done = bf16[16,4096]{1,0:T(8,128)(2,1)S(1)} collective-permute-done((bf16[16,4096]{1,0:T(8,128)(2,1)S(1)}, bf16[16,4096]{1,0:T(8,128)(2,1)S(1)}, u32[]{:S(2)}, u32[]{:S(2)}) %collective-permute-start) | collective-permute-done | bytes 131104 | tf_op jit(solution)/shard_map/while/body/eval_jaxpr/ppermute | solution.py:20
  256.4 7.9 %collective-permute-done = bf16[16,4096]{1,0:T(8,128)(2,1)S(1)} collective-permute-done((bf16[16,4096]{1,0:T(8,128)(2,1)S(1)}, bf16[16,4096]{1,0:T(8,128)(2,1)S(1)}, u32[]{:S(2)}, u32[]{:S(2)}) %collective-permute-start) | collective-permute-done | bytes 131104 | tf_op jit(solution)/shard_map/while/body/eval_jaxpr/ppermute | solution.py:20
  280.1 20.9 %subtract_convert_fusion = (bf16[64,2,64,1,32]{4,3,2,1,0:T(2,128)(2,1)S(1)}, bf16[64,2,64,1,32]{4,3,2,1,0:T(2,128)(2,1)S(1)}) fusion(f32[64,2,64]{2,1,0:T(2,128)S(1)} %copy.82, f32[64,64,32]{2,1,0:T(8,128)} %copy.81, f32[64,2,64]{2,1,0:T(2,128)S(1)} %copy.80, f32[64,64,32]{2,1,0:T(8,128)S(1)} %copy.68), kind=kLoop, calls=%fused_computation.24 | loop fusion | flops 2097152 | bytes 2162688 | tf_op jit(solution)/shard_map/convert.1
  301.0 12.0 %pad_maximum_fusion.1 = bf16[64,2,64,2,32]{4,3,2,1,0:T(2,128)(2,1)} fusion(bf16[64,2,64,1,32]{4,3,2,1,0:T(2,128)(2,1)S(1)} %get-tuple-element.307, bf16[64,2,64,1,32]{4,3,2,1,0:T(2,128)(2,1)S(1)} %get-tuple-element.306), kind=kLoop, calls=%fused_computation.22 | loop fusion | flops 2097152 | bytes 2097152 | tf_op jit(solution)/shard_map/stack | solution.py:42
  313.0 6.1 %convert_element_type.54 = bf16[128,4096]{1,0:T(8,128)(2,1)S(1)} reshape(bf16[64,2,64,2,32]{4,3,2,1,0:T(2,128)(2,1)} %pad_maximum_fusion.1) | data formatting | bytes 2097152 | tf_op jit(solution)/shard_map/convert_element_type | solution.py:105
  322.4 16.6 %all-to-all-start.1 = ((bf16[16,16,4096]{2,1,0:T(8,128)(2,1)}), bf16[16,16,4096]{2,1,0:T(8,128)(2,1)S(1)}, u32[]{:S(2)}, u32[]{:S(2)}) async-start(bf16[16,16,4096]{2,1,0:T(8,128)(2,1)} %bitcast.26), calls=%async_computation.1 | async-start | bytes 4194304 | tf_op jit(solution)/shard_map/all_to_all | solution.py:130
  339.3 25.8 %all-to-all-done.1 = bf16[16,16,4096]{2,1,0:T(8,128)(2,1)S(1)} async-done(((bf16[16,16,4096]{2,1,0:T(8,128)(2,1)}), bf16[16,16,4096]{2,1,0:T(8,128)(2,1)S(1)}, u32[]{:S(2)}, u32[]{:S(2)}) %all-to-all-start.1) | async-done | bytes 2097184 | tf_op jit(solution)/shard_map/all_to_all | solution.py:130
  366.6 109.2 %psum.7 = f32[256]{0:T(256)S(1)} all-reduce(f32[256]{0:T(256)S(1)} %select_reduce_fusion.2), channel_id=1, replica_groups=mesh['img'=32,'blk'=16] {'img','blk'}, use_global_device_ids=true, to_apply=%region_20.21 | all-reduce | flops 256 | bytes 2048 | tf_op jit(solution)/shard_map/psum | solution.py:109
  476.4 29.7 %reduce-scatter.2.cloned.1.call-done = f32[16,128]{1,0:T(8,128)} async-done(((f32[16,4096]{1,0:T(8,128)}), f32[16,128]{1,0:T(8,128)}) %reduce-scatter.2.cloned.1.call-update) | async-done | bytes 8208 | tf_op jit(solution)/shard_map/reduce_scatter | solution.py:138
  (585 shorter events, 162.3 us)
Async XLA Ops:
  7.2 19.2 %copy-start = (bf16[64,4096]{1,0:T(8,128)(2,1)S(1)}, bf16[64,4096]{1,0:T(8,128)(2,1)}, u32[]{:S(2)}) copy-start(bf16[64,4096]{1,0:T(8,128)(2,1)} %param.6) | copy-start | bytes 1572868
  13.3 309.2 %all-to-all-start = ((bf16[16,1,16]{2,1,0:T(2,128)(2,1)}), bf16[16,1,16]{2,1,0:T(2,128)(2,1)S(1)}, u32[]{:S(2)}, u32[]{:S(2)}) async-start(bf16[16,1,16]{2,1,0:T(2,128)(2,1)} %all_to_all.12), calls=%async_computation | async-start | bytes 16384 | tf_op jit(solution)/shard_map/all_to_all | solution.py:131
  30.6 4.4 copy-start.1
  31.7 5.0 copy-start.2
  37.2 6.3 %collective-permute-start = (bf16[16,4096]{1,0:T(8,128)(2,1)S(1)}, bf16[16,4096]{1,0:T(8,128)(2,1)S(1)}, u32[]{:S(2)}, u32[]{:S(2)}) collective-permute-start(bf16[16,4096]{1,0:T(8,128)(2,1)S(1)} %get-tuple-element.408), channel_id=1, source_target_pairs={{0,1},{1,2},{2,3},{3,4},{4,5},{5,6},{6,7},{7,8},{8,9},{9,10},{10,1... | collective-permute-start | bytes 393224 | tf_op jit(solution)/shard_map/while/body/eval_jaxpr/ppermute | solution.py:20
  50.0 6.3 %collective-permute-start = (bf16[16,4096]{1,0:T(8,128)(2,1)S(1)}, bf16[16,4096]{1,0:T(8,128)(2,1)S(1)}, u32[]{:S(2)}, u32[]{:S(2)}) collective-permute-start(bf16[16,4096]{1,0:T(8,128)(2,1)S(1)} %get-tuple-element.408), channel_id=1, source_target_pairs={{0,1},{1,2},{2,3},{3,4},{4,5},{5,6},{6,7},{7,8},{8,9},{9,10},{10,1... | collective-permute-start | bytes 393224 | tf_op jit(solution)/shard_map/while/body/eval_jaxpr/ppermute | solution.py:20
  62.7 6.3 %collective-permute-start = (bf16[16,4096]{1,0:T(8,128)(2,1)S(1)}, bf16[16,4096]{1,0:T(8,128)(2,1)S(1)}, u32[]{:S(2)}, u32[]{:S(2)}) collective-permute-start(bf16[16,4096]{1,0:T(8,128)(2,1)S(1)} %get-tuple-element.408), channel_id=1, source_target_pairs={{0,1},{1,2},{2,3},{3,4},{4,5},{5,6},{6,7},{7,8},{8,9},{9,10},{10,1... | collective-permute-start | bytes 393224 | tf_op jit(solution)/shard_map/while/body/eval_jaxpr/ppermute | solution.py:20
  75.4 8.9 %collective-permute-start = (bf16[16,4096]{1,0:T(8,128)(2,1)S(1)}, bf16[16,4096]{1,0:T(8,128)(2,1)S(1)}, u32[]{:S(2)}, u32[]{:S(2)}) collective-permute-start(bf16[16,4096]{1,0:T(8,128)(2,1)S(1)} %get-tuple-element.408), channel_id=1, source_target_pairs={{0,1},{1,2},{2,3},{3,4},{4,5},{5,6},{6,7},{7,8},{8,9},{9,10},{10,1... | collective-permute-start | bytes 393224 | tf_op jit(solution)/shard_map/while/body/eval_jaxpr/ppermute | solution.py:20
  90.8 9.9 %collective-permute-start = (bf16[16,4096]{1,0:T(8,128)(2,1)S(1)}, bf16[16,4096]{1,0:T(8,128)(2,1)S(1)}, u32[]{:S(2)}, u32[]{:S(2)}) collective-permute-start(bf16[16,4096]{1,0:T(8,128)(2,1)S(1)} %get-tuple-element.408), channel_id=1, source_target_pairs={{0,1},{1,2},{2,3},{3,4},{4,5},{5,6},{6,7},{7,8},{8,9},{9,10},{10,1... | collective-permute-start | bytes 393224 | tf_op jit(solution)/shard_map/while/body/eval_jaxpr/ppermute | solution.py:20
  107.1 9.9 %collective-permute-start = (bf16[16,4096]{1,0:T(8,128)(2,1)S(1)}, bf16[16,4096]{1,0:T(8,128)(2,1)S(1)}, u32[]{:S(2)}, u32[]{:S(2)}) collective-permute-start(bf16[16,4096]{1,0:T(8,128)(2,1)S(1)} %get-tuple-element.408), channel_id=1, source_target_pairs={{0,1},{1,2},{2,3},{3,4},{4,5},{5,6},{6,7},{7,8},{8,9},{9,10},{10,1... | collective-permute-start | bytes 393224 | tf_op jit(solution)/shard_map/while/body/eval_jaxpr/ppermute | solution.py:20
  123.5 9.9 %collective-permute-start = (bf16[16,4096]{1,0:T(8,128)(2,1)S(1)}, bf16[16,4096]{1,0:T(8,128)(2,1)S(1)}, u32[]{:S(2)}, u32[]{:S(2)}) collective-permute-start(bf16[16,4096]{1,0:T(8,128)(2,1)S(1)} %get-tuple-element.408), channel_id=1, source_target_pairs={{0,1},{1,2},{2,3},{3,4},{4,5},{5,6},{6,7},{7,8},{8,9},{9,10},{10,1... | collective-permute-start | bytes 393224 | tf_op jit(solution)/shard_map/while/body/eval_jaxpr/ppermute | solution.py:20
  139.8 9.9 %collective-permute-start = (bf16[16,4096]{1,0:T(8,128)(2,1)S(1)}, bf16[16,4096]{1,0:T(8,128)(2,1)S(1)}, u32[]{:S(2)}, u32[]{:S(2)}) collective-permute-start(bf16[16,4096]{1,0:T(8,128)(2,1)S(1)} %get-tuple-element.408), channel_id=1, source_target_pairs={{0,1},{1,2},{2,3},{3,4},{4,5},{5,6},{6,7},{7,8},{8,9},{9,10},{10,1... | collective-permute-start | bytes 393224 | tf_op jit(solution)/shard_map/while/body/eval_jaxpr/ppermute | solution.py:20
  156.2 9.9 %collective-permute-start = (bf16[16,4096]{1,0:T(8,128)(2,1)S(1)}, bf16[16,4096]{1,0:T(8,128)(2,1)S(1)}, u32[]{:S(2)}, u32[]{:S(2)}) collective-permute-start(bf16[16,4096]{1,0:T(8,128)(2,1)S(1)} %get-tuple-element.408), channel_id=1, source_target_pairs={{0,1},{1,2},{2,3},{3,4},{4,5},{5,6},{6,7},{7,8},{8,9},{9,10},{10,1... | collective-permute-start | bytes 393224 | tf_op jit(solution)/shard_map/while/body/eval_jaxpr/ppermute | solution.py:20
  172.6 9.9 %collective-permute-start = (bf16[16,4096]{1,0:T(8,128)(2,1)S(1)}, bf16[16,4096]{1,0:T(8,128)(2,1)S(1)}, u32[]{:S(2)}, u32[]{:S(2)}) collective-permute-start(bf16[16,4096]{1,0:T(8,128)(2,1)S(1)} %get-tuple-element.408), channel_id=1, source_target_pairs={{0,1},{1,2},{2,3},{3,4},{4,5},{5,6},{6,7},{7,8},{8,9},{9,10},{10,1... | collective-permute-start | bytes 393224 | tf_op jit(solution)/shard_map/while/body/eval_jaxpr/ppermute | solution.py:20
  188.9 9.9 %collective-permute-start = (bf16[16,4096]{1,0:T(8,128)(2,1)S(1)}, bf16[16,4096]{1,0:T(8,128)(2,1)S(1)}, u32[]{:S(2)}, u32[]{:S(2)}) collective-permute-start(bf16[16,4096]{1,0:T(8,128)(2,1)S(1)} %get-tuple-element.408), channel_id=1, source_target_pairs={{0,1},{1,2},{2,3},{3,4},{4,5},{5,6},{6,7},{7,8},{8,9},{9,10},{10,1... | collective-permute-start | bytes 393224 | tf_op jit(solution)/shard_map/while/body/eval_jaxpr/ppermute | solution.py:20
  205.3 9.9 %collective-permute-start = (bf16[16,4096]{1,0:T(8,128)(2,1)S(1)}, bf16[16,4096]{1,0:T(8,128)(2,1)S(1)}, u32[]{:S(2)}, u32[]{:S(2)}) collective-permute-start(bf16[16,4096]{1,0:T(8,128)(2,1)S(1)} %get-tuple-element.408), channel_id=1, source_target_pairs={{0,1},{1,2},{2,3},{3,4},{4,5},{5,6},{6,7},{7,8},{8,9},{9,10},{10,1... | collective-permute-start | bytes 393224 | tf_op jit(solution)/shard_map/while/body/eval_jaxpr/ppermute | solution.py:20
  221.6 9.9 %collective-permute-start = (bf16[16,4096]{1,0:T(8,128)(2,1)S(1)}, bf16[16,4096]{1,0:T(8,128)(2,1)S(1)}, u32[]{:S(2)}, u32[]{:S(2)}) collective-permute-start(bf16[16,4096]{1,0:T(8,128)(2,1)S(1)} %get-tuple-element.408), channel_id=1, source_target_pairs={{0,1},{1,2},{2,3},{3,4},{4,5},{5,6},{6,7},{7,8},{8,9},{9,10},{10,1... | collective-permute-start | bytes 393224 | tf_op jit(solution)/shard_map/while/body/eval_jaxpr/ppermute | solution.py:20
  238.0 9.9 %collective-permute-start = (bf16[16,4096]{1,0:T(8,128)(2,1)S(1)}, bf16[16,4096]{1,0:T(8,128)(2,1)S(1)}, u32[]{:S(2)}, u32[]{:S(2)}) collective-permute-start(bf16[16,4096]{1,0:T(8,128)(2,1)S(1)} %get-tuple-element.408), channel_id=1, source_target_pairs={{0,1},{1,2},{2,3},{3,4},{4,5},{5,6},{6,7},{7,8},{8,9},{9,10},{10,1... | collective-permute-start | bytes 393224 | tf_op jit(solution)/shard_map/while/body/eval_jaxpr/ppermute | solution.py:20
  254.3 9.9 %collective-permute-start = (bf16[16,4096]{1,0:T(8,128)(2,1)S(1)}, bf16[16,4096]{1,0:T(8,128)(2,1)S(1)}, u32[]{:S(2)}, u32[]{:S(2)}) collective-permute-start(bf16[16,4096]{1,0:T(8,128)(2,1)S(1)} %get-tuple-element.408), channel_id=1, source_target_pairs={{0,1},{1,2},{2,3},{3,4},{4,5},{5,6},{6,7},{7,8},{8,9},{9,10},{10,1... | collective-permute-start | bytes 393224 | tf_op jit(solution)/shard_map/while/body/eval_jaxpr/ppermute | solution.py:20
  322.4 42.6 %all-to-all-start.1 = ((bf16[16,16,4096]{2,1,0:T(8,128)(2,1)}), bf16[16,16,4096]{2,1,0:T(8,128)(2,1)S(1)}, u32[]{:S(2)}, u32[]{:S(2)}) async-start(bf16[16,16,4096]{2,1,0:T(8,128)(2,1)} %bitcast.26), calls=%async_computation.1 | async-start | bytes 4194304 | tf_op jit(solution)/shard_map/all_to_all | solution.py:130
  339.1 167.0 %reduce-scatter.2.cloned.1.call-start = ((), (), s32[]{:S(2)}) async-start(), calls=%async_computation.3 | async-start | bytes 270336 | tf_op jit(solution)/shard_map/reduce_scatter | solution.py:138
Sparse Core Ops, SparseCore 0:
  366.3 139.6 reduce-scatter.1
where the time goes:
time: 515 us; the launch traced here: 514 us
  waiting for transfers between devices  161 us (31%)
  blocking collectives  109 us (21%)
  other arithmetic  87.6 us (17%)
  local copies, waits for them, and re-layouts  63.9 us (12%)
  starting transfers between devices  54.7 us (11%)
  matrix products  20.8 us (4%)
  between operations  14.4 us (3%)
    psum x1, blocking collectives, body(): class_weight = lax.psum(local_weight, ('img', 'blk'))  109 us
    ppermute x15, waiting for transfers between devices, from_behind(): return lax.ppermute(x, axis, [(i, (i + by) % size) for i in range(size)])  106 us
    reduce_scatter x1, waiting for transfers between devices, body(): lax.psum_scatter(partial_sums, 'img', scatter_dimension=1, tiled=True)  29.7 us
    ppermute x15, starting transfers between devices, from_behind(): return lax.ppermute(x, axis, [(i, (i + by) % size) for i in range(size)])  28.9 us
    all_to_all x1, waiting for transfers between devices, body(): lax.all_to_all(send_rows, 'blk', split_axis=0, concat_axis=0, tiled=True)  25.8 us
    another operation x16, other arithmetic, block_scores(): swapped = jnp.stack([-pieces[:, :, 1, :], pieces[:, :, 0, :]], axis=2)  22 us
    another operation x2, other arithmetic  20.9 us
    neg x16, other arithmetic, block_scores(): swapped = jnp.stack([-pieces[:, :, 1, :], pieces[:, :, 0, :]], axis=2)  18.4 us
  transfers between devices with their start and end apart: 18, of which 17 were waited for; matrix products, arithmetic and copies ran while one was open for 32% of the time, Pallas kernels for 0%

commit v1 on v0

v1 whole, which is shorter than its diff:
```python
import math

import jax
import jax.numpy as jnp
import ml_dtypes
import numpy as np
from jax import lax
from jax.experimental import pallas as pl
from jax.experimental.pallas import tpu as pltpu
from jax.sharding import PartitionSpec as P

CYCLES = 32
ORDERS = 64
TURNS = 36
FEATS = 4096
LANES = 128
MESH = pl.DeviceIdType.MESH
F32 = jnp.float32
BF16 = jnp.bfloat16


def spread_table():
    feats = np.arange(FEATS)
    order = feats // (2 * CYCLES)
    turns = np.arange(TURNS)
    angle = 2.0 * math.pi / TURNS * ((turns[:, None] * order[None, :]) % TURNS)
    out = np.zeros((16, 128, 512), np.float32)
    for part, values in enumerate((np.cos(angle), -np.sin(angle))):
        values = values.astype(np.float32).reshape(TURNS, 16, 256).transpose(1, 0, 2)
        high = values.astype(ml_dtypes.bfloat16).astype(np.float32)
        low = values - high
        cols = slice(part * 256, part * 256 + 256)
        out[:, 0:36, cols] = high
        out[:, 40:76, cols] = high
        out[:, 80:116, cols] = low
    return out.astype(ml_dtypes.bfloat16)


def weighted(pairs):
    total = None
    for coef, value in pairs:
        if abs(coef) < 1e-12:
            continue
        if abs(coef - 1.0) < 1e-12:
            term = value
        elif abs(coef + 1.0) < 1e-12:
            term = -value
        else:
            term = value * np.float32(coef)
        total = term if total is None else total + term
    return total


def turns_of(a, b):
    def cos(k, s):
        return math.cos(2.0 * math.pi * (k * s % 36) / 36.0)

    def sin(k, s):
        return math.sin(2.0 * math.pi * (k * s % 36) / 36.0)

    even_c, odd_c, even_s, odd_s = {}, {}, {}, {}
    for s in range(5):
        p = weighted([(cos(k, s), a[k]) for k in range(0, 19, 4)])
        q = weighted([(cos(k, s), a[k]) for k in range(2, 19, 4)])
        even_c[s], even_c[9 - s] = p + q, p - q
    for s in range(9):
        odd_c[s] = weighted([(cos(k, s), a[k]) for k in range(1, 18, 2)])
    for s in range(1, 5):
        p = weighted([(sin(k, s), b[k]) for k in range(4, 17, 4)])
        q = weighted([(sin(k, s), b[k]) for k in range(2, 17, 4)])
        even_s[s], even_s[9 - s] = p + q, q - p
    for s in range(1, 10):
        odd_s[s] = weighted([(sin(k, s), b[k]) for k in range(1, 18, 2)])
    x = [None] * 36
    for s in range(10):
        if s < 9:
            c_lo, c_hi = even_c[s] + odd_c[s], even_c[s] - odd_c[s]
        else:
            c_lo = c_hi = even_c[9]
        if s == 0:
            x[0], x[18] = c_lo, c_hi
        elif s == 9:
            x[9], x[27] = c_lo - odd_s[9], c_lo + odd_s[9]
        else:
            s_lo, s_hi = even_s[s] + odd_s[s], odd_s[s] - even_s[s]
            x[s], x[36 - s] = c_lo - s_lo, c_lo + s_lo
            x[18 - s], x[18 + s] = c_hi - s_hi, c_hi + s_hi
    return x


def tree(op, values):
    values = list(values)
    while len(values) > 1:
        nxt = [op(values[i], values[i + 1]) for i in range(0, len(values) - 1, 2)]
        if len(values) % 2:
            nxt.append(values[-1])
        values = nxt
    return values[0]


def add(p, q):
    return p + q


def dot_nt(a, b, **kw):
    return lax.dot_general(a, b, (((1,), (1,)), ((), ())), preferred_element_type=F32, **kw)


def dot_nn(a, b):
    return jnp.dot(a, b, preferred_element_type=F32)


def kernel(
    images, refs, aux, table, avg_out, evid_out,
    G, IM, IMS, FI, F, AUXS, CHX, CHS, PT, PP, TE, OH, SA, RA, SB, RB, TA, R2A, TB, R2B,
    UZ, SZ, RZ, W0, RW0, W1, RW1, W2, RW2, LS, LR,
    loc, ags, agr, sibs, sibr, s1s, s1r, s2s, s2r, zs, zr, ws, wr,
):
    img, blk = lax.axis_index("img"), lax.axis_index("blk")
    z, x_lo = img % 16, img // 16
    core, y, x_hi = blk % 2, (blk // 2) % 4, blk // 8
    x = x_hi * 2 + x_lo
    q_me = x_hi * 4 + y

    def dev(x_, y_, z_, c_):
        return ((x_ % 2) * 16 + z_, (x_ // 2) * 8 + y_ * 2 + c_)

    sib = dev(x, y, z, 1 - core)
    y_up, y_dn = (y + 1) % 4, (y + 3) % 4
    up, down = dev(x, y_up, z, core), dev(x, y_dn, z, core)
    x_opp, x_same = 3 - x, x_hi * 2 + 1 - x_lo
    opp, same = dev(x_opp, y, z, core), dev(x_same, y, z, core)

    def at_y(d):
        return dev(x, (y + d) % 4, z, core)

    def at_x(d):
        return dev((x + d) % 4, y, z, core)

    def at_z(d):
        return dev(x, y, (z + d) % 16, core)

    sent = []

    def send(src, dst, ssem, rsem, to):
        copy = pltpu.make_async_remote_copy(
            src_ref=src, dst_ref=dst, send_sem=ssem, recv_sem=rsem, device_id=to, device_id_type=MESH
        )
        copy.start()
        sent.append(copy)

    def arrived(dst, rsem):
        pltpu.make_async_copy(dst, dst, rsem).wait()

    mine_rows = pl.ds(pl.multiple_of(core * 64, 64), 64)
    own_im = pltpu.make_async_copy(images, IM.at[mine_rows], loc.at[0])
    own_im.start()
    own_g = pltpu.make_async_copy(refs, G.at[pl.ds(pl.multiple_of(q_me * 16, 16), 16)], loc.at[1])
    own_g.start()
    own_t = pltpu.make_async_copy(table, TE, loc.at[2])
    own_t.start()

    barrier = pltpu.get_barrier_semaphore()
    partners = [sib] + [at_y(d) for d in range(1, 4)] + [at_x(d) for d in range(1, 4)]
    partners += [at_z(d) for d in range(1, 16)]
    for to in partners:
        pl.semaphore_signal(barrier, inc=1, device_id=to, device_id_type=MESH)
    pl.semaphore_wait(barrier, len(partners))

    def piece(q, h):
        return G.at[pl.ds(pl.multiple_of(q * 16, 16), 16), pl.ds(pl.multiple_of(h * 2048, 2048), 2048)]

    def own_piece(h):
        return refs.at[:, pl.ds(pl.multiple_of(h * 2048, 2048), 2048)]

    h = x_lo
    col, far = x_hi * 4, (1 - x_hi) * 4
    y_far = (y + 2) % 4

    def give(n, q, hh, to, src=None):
        send(piece(q, hh) if src is None else src, piece(q, hh), ags.at[n], agr.at[q, hh], to)

    def got(q, hh):
        arrived(piece(q, hh), agr.at[q, hh])

    give(0, q_me, 0, up, own_piece(0))
    give(1, q_me, 1, down, own_piece(1))
    give(2, q_me, h, opp, own_piece(h))
    give(3, q_me, 1, up, own_piece(1))
    give(4, q_me, 0, down, own_piece(0))
    send(images, IM.at[mine_rows], sibs.at[0], sibr.at[0], sib)
    send(aux, AUXS, sibs.at[1], sibr.at[1], sib)
    own_im.wait()
    arrived(IM.at[pl.ds(pl.multiple_of((1 - core) * 64, 64), 64)], sibr.at[0])
    arrived(AUXS, sibr.at[1])

    row = lax.broadcasted_iota(jnp.int32, (128, 128), 0)
    lane = lax.broadcasted_iota(jnp.int32, (128, 128), 1)

    def swap(src, dst):
        first = dst % 64 < 32
        return jnp.where(first & (src == dst + 32), 1.0, jnp.where((~first) & (src == dst - 32), -1.0, 0.0))

    eye = jnp.where(row == lane, 1.0, 0.0)
    rows_of = jnp.concatenate([eye, swap(lane, row)], axis=0).astype(BF16)
    cols_of = swap(row, lane).astype(BF16)

    def prepare(first, count, half):
        def step(n, carry):
            t = first + n
            block = IM[:, pl.ds(pl.multiple_of(t * 128, 128), 128)]
            both = dot_nt(rows_of, block)
            j = t - 18 * half
            sign = jnp.where(j < 9, 1.0, -1.0).astype(F32)
            FI[j, half * 128 : half * 128 + 128, 0:128] = both[0:128].astype(BF16)
            FI[j, half * 128 : half * 128 + 128, 128:256] = (both[128:256] * sign).astype(BF16)
            IMS[:, pl.ds(pl.multiple_of(t * 128, 128), 128)] = dot_nn(block, cols_of).astype(BF16)
            return carry

        lax.fori_loop(0, count, step, 0)

    prepare(0, 6, 0)
    got(col + y_dn, 0)
    give(5, col + y_dn, 0, up)
    got(col + y_up, 1)
    give(6, col + y_up, 1, down)
    prepare(6, 6, 0)
    got(col + y_dn, 1)
    got(col + y_up, 0)
    give(7, col + y_dn, h, opp)
    give(8, col + y_up, h, opp)
    got(far + y, 1 - h)
    give(9, far + y, 1 - h, same)
    prepare(12, 6, 0)
    got(col + y_far, 0)
    got(col + y_far, 1)
    give(10, col + y_far, h, opp)
    prepare(18, 7, 1)
    got(far + y_dn, 1 - h)
    give(11, far + y_dn, 1 - h, same)
    got(far + y_up, 1 - h)
    give(12, far + y_up, 1 - h, same)
    prepare(25, 7, 1)
    got(far + y_far, 1 - h)
    give(13, far + y_far, 1 - h, same)

    right = lax.broadcasted_iota(jnp.int32, (8, 128), 1) >= 64
    auxc = jnp.where(right == (core == 1), aux[...], AUXS[...])
    precision = auxc[0:1, :]
    class_id = ((row // 16) * 32 + core * 16 + row % 16).astype(F32)
    picks = [auxc[1:2, :] == class_id, auxc[2:3, :] == class_id]
    for k in range(2):
        OH[:, k * 128 : k * 128 + 128] = jnp.where(picks[k], 1.0, 0.0).astype(BF16)
    PT[...] = jnp.zeros_like(PT)

    for d in (0, 1, 2, 3):
        got(far + (y + d) % 4, h)
    own_g.wait()

    low = (lax.broadcasted_iota(jnp.int32, (128, 256), 1) % 128) < 64
    for j in range(18):
        left = G[:, j * 128 : j * 128 + 128]
        if j < 14:
            tile = jnp.concatenate([left, G[:, (18 + j) * 128 : (18 + j) * 128 + 128]], axis=1)
            keep, right_side = low, FI[j]
        else:
            tile, keep, right_side = left, low[:, 0:128], FI[j, 0:128, :]
        zero = jnp.zeros_like(tile)
        stacked = jnp.concatenate([jnp.where(keep, tile, zero), jnp.where(keep, zero, tile)], axis=0)
        out = dot_nn(stacked, right_side)
        even, odd = out[0:128], out[128:256]
        k_even, k_odd = (2 * j if j <= 9 else 36 - 2 * j), (2 * j + 1 if j <= 8 else 35 - 2 * j)
        if j <= 9:
            F[k_even] = even[:, 0:128]
        else:
            F[k_even] += even[:, 0:128]
        if 0 < k_even < 18:
            if j <= 9:
                F[18 + k_even] = even[:, 128:256]
            else:
                F[18 + k_even] += even[:, 128:256]
        if j <= 8:
            F[k_odd] = odd[:, 0:128]
            F[18 + k_odd] = odd[:, 128:256]
        else:
            F[k_odd] += odd[:, 0:128]
            F[18 + k_odd] += odd[:, 128:256]

    square = jnp.zeros((128, 128), F32)
    for t in range(32):
        value = G[:, t * 128 : t * 128 + 128].astype(F32)
        square = square + value * value
    F[36] = jnp.broadcast_to(0.5 * jnp.sum(square, axis=1, keepdims=True), (128, 128))

    even_row = lax.broadcasted_iota(jnp.int32, (8, 128), 0) % 2 == 0

    def choose(kk, carry):
        f = F[kk]
        parts = []
        for k in range(2):
            kept = jnp.where(picks[k], f, 0.0)
            total = tree(add, [kept[n * 8 : n * 8 + 8] for n in range(16)])
            parts.append(total + pltpu.roll(total, 1, 0))
        both = jnp.where(even_row, parts[0], parts[1])
        both = both + pltpu.roll(both, 2, 0)
        CHX[kk] = both + pltpu.roll(both, 4, 0)
        return carry

    lax.fori_loop(0, 37, choose, 0)
    send(CHX, CHS, sibs.at[2], sibr.at[2], sib)
    arrived(CHS, sibr.at[2])

    coefs = [CHX[k] + CHS[k] for k in range(37)]
    turned = turns_of(coefs[0:19], [None] + coefs[19:36])
    scores = [precision * (v - coefs[36]) for v in turned]
    peak = tree(jnp.maximum, scores)
    peak = jnp.maximum(peak, jnp.where(even_row, pltpu.roll(peak, 7, 0), pltpu.roll(peak, 1, 0)))
    exps = [jnp.exp(v - peak) for v in scores]
    total = tree(add, exps)
    total = total + jnp.where(even_row, pltpu.roll(total, 7, 0), pltpu.roll(total, 1, 0))
    posterior = [v / total for v in exps]
    share = tree(add, posterior)
    for s in range(TURNS):
        high = posterior[s].astype(BF16).astype(F32)
        rest = posterior[s] - high
        for k in range(2):
            PT[k, s : s + 1, :] = high[k : k + 1]
            PT[k, 40 + s : 41 + s, :] = rest[k : k + 1]
            PT[k, 80 + s : 81 + s, :] = high[k : k + 1]
    for k in range(2):
        PP[k * 128 : k * 128 + 128, :] = PT[k].T.astype(BF16)
    own_t.wait()

    onehot = OH[...]

    def sums(x_half, second):
        def step(v, carry):
            u = x_half * 8 + second * 4 + v
            lanes = pl.ds(pl.multiple_of(u * 256, 256), 256)
            out_lanes = pl.ds(pl.multiple_of(v * 256, 256), 256)
            factor = dot_nn(PP[...], TE[u])
            straight, turned_in = IM[:, lanes].astype(F32), IMS[:, lanes].astype(F32)
            rows = [
                (
                    straight * factor[k * 128 : k * 128 + 128, 0:256]
                    - turned_in * factor[k * 128 : k * 128 + 128, 256:512]
                ).astype(BF16)
                for k in range(2)
            ]
            out = dot_nn(onehot, jnp.concatenate(rows, axis=0)).astype(BF16)
            for q in range(8):
                block = out[q * 16 : q * 16 + 16]
                if second:
                    SB[(q // 4) * 2 + x_half, q % 4, :, out_lanes] = block
                else:
                    SA[x_half, q % 4, q // 4, :, out_lanes] = block
            return carry

        lax.fori_loop(0, 4, step, 0)

    for x_half in range(2):
        sums(x_half, 0)
        for d in range(1, 4):
            n = x_half * 3 + d - 1
            send(SA.at[x_half, (y + d) % 4], RA.at[d - 1, x_half], s1s.at[n], s1r.at[n], at_y(d))
    for x_half in range(2):
        sums(x_half, 1)
    for d in range(1, 4):
        n = 5 + d
        send(SB.at[(x + d) % 4], RB.at[d - 1], s1s.at[n], s1r.at[n], at_x(d))

    shares = jnp.concatenate(
        [jnp.broadcast_to(share[0:1], (8, 128)), jnp.broadcast_to(share[1:2], (8, 128))], axis=1
    )
    W0[...] = dot_nt(shares, onehot.astype(F32), precision=lax.Precision.HIGHEST)
    for d in range(1, 16):
        send(W0, RW0.at[d - 1], ws.at[d - 1], wr.at[d - 1], at_z(d))

    def block_scores(n, carry):
        run_peak, run_total = carry
        rows = pl.ds(pl.multiple_of(n * 8, 8), 8)
        f = [F[k, rows, :] for k in range(37)]
        turned = turns_of(f[0:19], [None] + f[19:36])
        scores = [precision * (v - f[36]) for v in turned]
        new_peak = jnp.maximum(run_peak, tree(jnp.maximum, scores))
        total = tree(add, [jnp.exp(v - new_peak) for v in scores])
        return new_peak, run_total * jnp.exp(run_peak - new_peak) + total

    start = (jnp.full((8, 128), -jnp.inf, F32), jnp.zeros((8, 128), F32))
    run_peak, run_total = lax.fori_loop(0, 16, block_scores, start)
    peak = jnp.max(run_peak, axis=0, keepdims=True)
    total = jnp.sum(run_total * jnp.exp(run_peak - peak), axis=0, keepdims=True)
    LS[0:8] = jnp.broadcast_to(peak, (8, 128))
    LS[8:16] = jnp.broadcast_to(total, (8, 128))
    send(LS, LR, sibs.at[3], sibr.at[3], sib)

    for d in range(1, 16):
        arrived(RW0.at[d - 1], wr.at[d - 1])
    W1[...] = tree(add, [W0[...]] + [RW0[d] for d in range(15)])
    for d in range(1, 4):
        send(W1, RW1.at[d - 1], ws.at[14 + d], wr.at[14 + d], at_y(d))

    for d in range(1, 4):
        for x_half in range(2):
            arrived(RA.at[d - 1, x_half], s1r.at[x_half * 3 + d - 1])
    for x_half in range(2):
        for x_top in range(2):
            total = SA[x_half, y, x_top].astype(F32)
            for d in range(3):
                total = total + RA[d, x_half, x_top].astype(F32)
            TA[x_top * 2 + x_half] = total
    for d in range(1, 4):
        send(TA.at[(x + d) % 4], R2A.at[d - 1], s2s.at[d - 1], s2r.at[d - 1], at_x(d))
    for d in range(1, 4):
        arrived(RB.at[d - 1], s1r.at[5 + d])
    for y_to in range(4):
        total = SB[x, y_to].astype(F32)
        for d in range(3):
            total = total + RB[d, y_to].astype(F32)
        TB[y_to] = total
    for d in range(1, 4):
        send(TB.at[(y + d) % 4], R2B.at[d - 1], s2s.at[2 + d], s2r.at[2 + d], at_y(d))

    for d in range(1, 4):
        arrived(RW1.at[d - 1], wr.at[14 + d])
    W2[...] = tree(add, [W1[...]] + [RW1[d] for d in range(3)])
    for d in range(1, 4):
        send(W2, RW2.at[d - 1], ws.at[17 + d], wr.at[17 + d], at_x(d))

    arrived(LR, sibr.at[3])
    peak = jnp.maximum(LS[0:8], LR[0:8])
    total = LS[8:16] * jnp.exp(LS[0:8] - peak) + LR[8:16] * jnp.exp(LR[0:8] - peak)
    evidence = peak + jnp.log(total)
    evid_out[...] = jnp.where(core == 0, evidence[0:1, 0:64], evidence[0:1, 64:128])

    for d in range(1, 4):
        arrived(R2A.at[d - 1], s2r.at[d - 1])
    total = TA[x] + R2A[0] + R2A[1] + R2A[2]
    for n in range(8):
        UZ[n] = total[:, n * 128 : n * 128 + 128]
    for d in range(1, 4):
        arrived(R2B.at[d - 1], s2r.at[2 + d])
    total = TB[y] + R2B[0] + R2B[1] + R2B[2]
    for n in range(8):
        UZ[8 + n] = total[:, n * 128 : n * 128 + 128]
    SZ[...] = UZ[...].astype(BF16)
    for d in range(1, 16):
        send(SZ.at[(z + d) % 16], RZ.at[d - 1], zs.at[d - 1], zr.at[d - 1], at_z(d))

    for d in range(1, 4):
        arrived(RW2.at[d - 1], wr.at[17 + d])
    weight = tree(add, [W2[...]] + [RW2[d] for d in range(3)])
    pick = lane[0:16] == row[0:16] + q_me * 16
    weight = jnp.sum(jnp.where(pick, jnp.broadcast_to(weight[0:1], (16, 128)), 0.0), axis=1, keepdims=True)
    for d in range(1, 16):
        arrived(RZ.at[d - 1], zr.at[d - 1])
    total = tree(add, [UZ[z]] + [RZ[d].astype(F32) for d in range(15)])
    avg_out[...] = total / (1.0 + weight)
    for copy in sent:
        copy.wait_send()


def body(images, references, precision, candidates):
    rows = jnp.concatenate(
        [precision.reshape(1, 64), candidates.T.astype(F32), jnp.zeros((5, 64), F32)], axis=0
    )
    aux = jnp.concatenate([rows, rows], axis=1)
    table = jnp.asarray(spread_table())
    anywhere = pl.BlockSpec(memory_space=pl.ANY)
    vmem = pl.BlockSpec(memory_space=pltpu.VMEM)
    dma = pltpu.SemaphoreType.DMA
    scratch = [
        pltpu.VMEM((128, 4096), BF16),
        pltpu.VMEM((128, 4096), BF16),
        pltpu.VMEM((128, 4096), BF16),
        pltpu.VMEM((18, 256, 256), BF16),
        pltpu.VMEM((37, 128, 128), F32),
        pltpu.VMEM((8, 128), F32),
        pltpu.VMEM((37, 8, 128), F32),
        pltpu.VMEM((37, 8, 128), F32),
        pltpu.VMEM((2, 128, 128), F32),
        pltpu.VMEM((256, 128), BF16),
        pltpu.VMEM((16, 128, 512), BF16),
        pltpu.VMEM((128, 256), BF16),
        pltpu.VMEM((2, 4, 2, 16, 1024), BF16),
        pltpu.VMEM((3, 2, 2, 16, 1024), BF16),
        pltpu.VMEM((4, 4, 16, 1024), BF16),
        pltpu.VMEM((3, 4, 16, 1024), BF16),
        pltpu.VMEM((4, 16, 1024), F32),
        pltpu.VMEM((3, 16, 1024), F32),
        pltpu.VMEM((4, 16, 1024), F32),
        pltpu.VMEM((3, 16, 1024), F32),
        pltpu.VMEM((16, 16, 128), F32),
        pltpu.VMEM((16, 16, 128), BF16),
        pltpu.VMEM((15, 16, 128), BF16),
        pltpu.VMEM((8, 128), F32),
        pltpu.VMEM((15, 8, 128), F32),
        pltpu.VMEM((8, 128), F32),
        pltpu.VMEM((3, 8, 128), F32),
        pltpu.VMEM((8, 128), F32),
        pltpu.VMEM((3, 8, 128), F32),
        pltpu.VMEM((16, 128), F32),
        pltpu.VMEM((16, 128), F32),
        dma((3,)),
        dma((14,)),
        dma((8, 2)),
        dma((4,)),
        dma((4,)),
        dma((9,)),
        dma((9,)),
        dma((6,)),
        dma((6,)),
        dma((15,)),
        dma((15,)),
        dma((21,)),
        dma((21,)),
    ]
    average, evidence = pl.pallas_call(
        kernel,
        out_shape=(jax.ShapeDtypeStruct((16, 128), F32), jax.ShapeDtypeStruct((1, 64), F32)),
        in_specs=[anywhere, anywhere, vmem, anywhere],
        out_specs=(vmem, vmem),
        scratch_shapes=scratch,
        compiler_params=pltpu.CompilerParams(
            collective_id=0, has_side_effects=True, vmem_limit_bytes=40 * 1024 * 1024
        ),
    )(images, references, aux, table)
    return average, evidence.reshape(64)


def solution(mesh):
    in_specs = (P(("img", "blk"), None), P("blk", None), P(("img", "blk")), P(("img", "blk"), None))
    out_specs = (P("blk", "img"), P(("img", "blk")))
    return jax.shard_map(body, mesh=mesh, in_specs=in_specs, out_specs=out_specs, check_vma=False)
```

time: 515 us -> 73 us (0.14)
  the two profiles are of different devices: /device:TPU:12 before, /device:TPU:1 now
where the time goes in v1:
time: 73 us; the launch traced here: 71.9 us
  Pallas kernels  65.1 us (89%)
  local copies, waits for them, and re-layouts  4.65 us (6%)
  other arithmetic  1.49 us (2%)
    pallas_call x1, Pallas kernels, body(): pl.pallas_call(kernel, out_shape=(jax.ShapeDtypeStruct((16, 128), F32), j...  65.1 us
    unnamed x8, local copies, waits for them, and re-layouts  4.65 us

profile of v1, /device:TPU:1, one launch (start us, length us, event | category | flops | bytes accessed | tf_op | source)
XLA Modules:
  0.0 71.9 jit_solution(13277408121985901569)
XLA Ops:
  0.6 0.7 convert_bitcast_fusion
  1.3 0.8 %maximum_maximum_fusion.aux = f32[8,128]{1,0:T(8,128)S(1)} fusion(f32[5,64]{1,0:T(8,128)S(1)} %broadcast_in_dim.3, f32[2,64]{1,0:T(2,128)S(1)} %convert_bitcast_fusion, f32[1,64]{1,0:T(1,128)} %bitcast.5), kind=kLoop, calls=%fused_computation | loop fusion | flops 5120 | bytes 6144 | tf_op jit(solution)/shard_map/concatenate | solution.py:467
  2.1 0.0 copy-start
  2.1 1.6 %copy-done = bf16[16,128,512]{2,1,0:T(8,128)(2,1)S(1)} copy-done((bf16[16,128,512]{2,1,0:T(8,128)(2,1)S(1)}, bf16[16,128,512]{2,1,0:T(8,128)(2,1)}, u32[]{:S(2)}) %copy-start) | copy-done | bytes 2097176
  3.7 0.0 copy-start.1
  3.7 1.0 %copy-done.1 = bf16[64,4096]{1,0:T(8,128)(2,1)S(1)} copy-done((bf16[64,4096]{1,0:T(8,128)(2,1)S(1)}, bf16[64,4096]{1,0:T(8,128)(2,1)}, u32[]{:S(2)}) %copy-start.1) | copy-done | bytes 524312
  4.8 0.0 copy-start.2
  4.8 0.9 %copy-done.2 = bf16[16,4096]{1,0:T(8,128)(2,1)S(1)} copy-done((bf16[16,4096]{1,0:T(8,128)(2,1)S(1)}, bf16[16,4096]{1,0:T(8,128)(2,1)}, u32[]{:S(2)}) %copy-start.2) | copy-done | bytes 131096
  5.7 65.1 %shard_map.68 = (f32[16,128]{1,0:T(8,128)S(1)}, f32[1,64]{1,0:T(1,128)S(1)}) custom-call(bf16[64,4096]{1,0:T(8,128)(2,1)S(1)} %copy-done.1, bf16[16,4096]{1,0:T(8,128)(2,1)S(1)} %copy-done.2, f32[8,128]{1,0:T(8,128)S(1)} %maximum_maximum_fusion.aux, bf16[16,128,512]{2,1,0:T(8,128)(2,1)S(1)} %copy-done), custom_call_target="tpu_custom_call" | custom-call | tf_op jit(solution)/shard_map/pallas_call | solution.py:518
  70.8 0.6 copy.9
  71.4 0.5 copy.10
  (1 shorter events, 0.0 us)
Async XLA Ops:
  2.1 1.6 %copy-start = (bf16[16,128,512]{2,1,0:T(8,128)(2,1)S(1)}, bf16[16,128,512]{2,1,0:T(8,128)(2,1)}, u32[]{:S(2)}) copy-start(bf16[16,128,512]{2,1,0:T(8,128)(2,1)} %constant.4.clone.table) | copy-start | bytes 6291460
  3.7 1.0 %copy-start.1 = (bf16[64,4096]{1,0:T(8,128)(2,1)S(1)}, bf16[64,4096]{1,0:T(8,128)(2,1)}, u32[]{:S(2)}) copy-start(bf16[64,4096]{1,0:T(8,128)(2,1)} %images.1) | copy-start | bytes 1572868
  4.8 0.9 %copy-start.2 = (bf16[16,4096]{1,0:T(8,128)(2,1)S(1)}, bf16[16,4096]{1,0:T(8,128)(2,1)}, u32[]{:S(2)}) copy-start(bf16[16,4096]{1,0:T(8,128)(2,1)} %refs.1) | copy-start | bytes 393220

commit v2 on v1

--- a/solution.py
+++ b/solution.py
@@ -111,10 +111,10 @@
 
 
 def kernel(
-    images, refs, aux, table, avg_out, evid_out,
-    G, IM, IMS, FI, F, AUXS, CHX, CHS, PT, PP, TE, OH, SA, RA, SB, RB, TA, R2A, TB, R2B,
+    images, refs, prec, cand, table, avg_out, evid_out,
+    G, IM, IMS, FI, F, PIN, CIN, AUX, AUXS, CHX, CHS, PT, PP, TE, OH, SA, RA, SB, RB, TA, R2A, TB, R2B,
     UZ, SZ, RZ, W0, RW0, W1, RW1, W2, RW2, LS, LR,
-    loc, ags, agr, sibs, sibr, s1s, s1r, s2s, s2r, zs, zr, ws, wr,
+    loc, tok, ags, agr, sibs, sibr, s1s, s1r, s2s, s2r, zs, zr, ws, wr,
 ):
     img, blk = lax.axis_index("img"), lax.axis_index("blk")
     z, x_lo = img % 16, img // 16
@@ -126,10 +126,8 @@
         return ((x_ % 2) * 16 + z_, (x_ // 2) * 8 + y_ * 2 + c_)
 
     sib = dev(x, y, z, 1 - core)
-    y_up, y_dn = (y + 1) % 4, (y + 3) % 4
-    up, down = dev(x, y_up, z, core), dev(x, y_dn, z, core)
     x_opp, x_same = 3 - x, x_hi * 2 + 1 - x_lo
-    opp, same = dev(x_opp, y, z, core), dev(x_same, y, z, core)
+    same = dev(x_same, y, z, core)
 
     def at_y(d):
         return dev(x, (y + d) % 4, z, core)
@@ -153,43 +151,58 @@
         pltpu.make_async_copy(dst, dst, rsem).wait()
 
     mine_rows = pl.ds(pl.multiple_of(core * 64, 64), 64)
+    own_p = pltpu.make_async_copy(prec, PIN, loc.at[3])
+    own_p.start()
+    own_c = pltpu.make_async_copy(cand, CIN, loc.at[4])
+    own_c.start()
+    own_g = pltpu.make_async_copy(refs, G.at[pl.ds(pl.multiple_of(q_me * 16, 16), 16)], loc.at[1])
+    own_g.start()
     own_im = pltpu.make_async_copy(images, IM.at[mine_rows], loc.at[0])
     own_im.start()
-    own_g = pltpu.make_async_copy(refs, G.at[pl.ds(pl.multiple_of(q_me * 16, 16), 16)], loc.at[1])
-    own_g.start()
     own_t = pltpu.make_async_copy(table, TE, loc.at[2])
     own_t.start()
 
     barrier = pltpu.get_barrier_semaphore()
-    partners = [sib] + [at_y(d) for d in range(1, 4)] + [at_x(d) for d in range(1, 4)]
-    partners += [at_z(d) for d in range(1, 16)]
+    partners = [dev(x_opp, (y + d) % 4, z, core) for d in range(1, 4)]
+    partners += [at_y(d) for d in range(1, 4)] + [at_x(d) for d in range(1, 4)]
+    partners += [at_z(1), at_z(15), sib]
     for to in partners:
         pl.semaphore_signal(barrier, inc=1, device_id=to, device_id_type=MESH)
+    own_p.wait()
+    own_c.wait()
+    mine = jnp.concatenate([PIN[...], CIN[...].astype(F32)], axis=0)
+    AUX[0:3, :] = jnp.concatenate([mine, mine], axis=1)
+    AUX[3:8, :] = jnp.zeros((5, 128), F32)
     pl.semaphore_wait(barrier, len(partners))
 
-    def piece(q, h):
-        return G.at[pl.ds(pl.multiple_of(q * 16, 16), 16), pl.ds(pl.multiple_of(h * 2048, 2048), 2048)]
-
-    def own_piece(h):
-        return refs.at[:, pl.ds(pl.multiple_of(h * 2048, 2048), 2048)]
+    def token(n):
+        for d in (1 << n, 16 - (1 << n)):
+            pl.semaphore_signal(tok.at[n], inc=1, device_id=at_z(d), device_id_type=MESH)
+
+    def rows_at(q):
+        return pl.ds(pl.multiple_of(q * 16, 16), 16)
+
+    def piece(q, hh):
+        return G.at[rows_at(q), pl.ds(pl.multiple_of(hh * 2048, 2048), 2048)]
 
     h = x_lo
     col, far = x_hi * 4, (1 - x_hi) * 4
-    y_far = (y + 2) % 4
-
-    def give(n, q, hh, to, src=None):
-        send(piece(q, hh) if src is None else src, piece(q, hh), ags.at[n], agr.at[q, hh], to)
-
-    def got(q, hh):
-        arrived(piece(q, hh), agr.at[q, hh])
-
-    give(0, q_me, 0, up, own_piece(0))
-    give(1, q_me, 1, down, own_piece(1))
-    give(2, q_me, h, opp, own_piece(h))
-    give(3, q_me, 1, up, own_piece(1))
-    give(4, q_me, 0, down, own_piece(0))
+    order = (0, 1, 3, 2)
+
+    def near_q(d):
+        return col + (y + d) % 4
+
+    def far_q(d):
+        return far + (y + d) % 4
+
+    send(AUX, AUXS, sibs.at[1], sibr.at[1], sib)
     send(images, IM.at[mine_rows], sibs.at[0], sibr.at[0], sib)
-    send(aux, AUXS, sibs.at[1], sibr.at[1], sib)
+    own_half = refs.at[:, pl.ds(pl.multiple_of(h * 2048, 2048), 2048)]
+    for n, d in enumerate(order):
+        send(own_half, piece(q_me, h), ags.at[n], agr.at[q_me, h], dev(x_opp, (y + d) % 4, z, core))
+    for n, d in enumerate((1, 3, 2)):
+        send(refs, G.at[rows_at(q_me)], ags.at[4 + n], agr.at[q_me, 0], at_y(d))
+    token(0)
     own_im.wait()
     arrived(IM.at[pl.ds(pl.multiple_of((1 - core) * 64, 64), 64)], sibr.at[0])
     arrived(AUXS, sibr.at[1])
@@ -217,35 +230,27 @@
             IMS[:, pl.ds(pl.multiple_of(t * 128, 128), 128)] = dot_nn(block, cols_of).astype(BF16)
             return carry
 
-        lax.fori_loop(0, count, step, 0)
-
-    prepare(0, 6, 0)
-    got(col + y_dn, 0)
-    give(5, col + y_dn, 0, up)
-    got(col + y_up, 1)
-    give(6, col + y_up, 1, down)
-    prepare(6, 6, 0)
-    got(col + y_dn, 1)
-    got(col + y_up, 0)
-    give(7, col + y_dn, h, opp)
-    give(8, col + y_up, h, opp)
-    got(far + y, 1 - h)
-    give(9, far + y, 1 - h, same)
-    prepare(12, 6, 0)
-    got(col + y_far, 0)
-    got(col + y_far, 1)
-    give(10, col + y_far, h, opp)
-    prepare(18, 7, 1)
-    got(far + y_dn, 1 - h)
-    give(11, far + y_dn, 1 - h, same)
-    got(far + y_up, 1 - h)
-    give(12, far + y_up, 1 - h, same)
-    prepare(25, 7, 1)
-    got(far + y_far, 1 - h)
-    give(13, far + y_far, 1 - h, same)
+        lax.fori_loop(0, count, step, 0, unroll=2)
+
+    def forward(n):
+        q = far_q(order[n])
+        arrived(piece(q, 1 - h), agr.at[q, 1 - h])
+        send(piece(q, 1 - h), piece(q, 1 - h), ags.at[7 + n], agr.at[q, 1 - h], same)
+
+    prepare(0, 8, 0)
+    forward(0)
+    prepare(8, 4, 0)
+    forward(1)
+    prepare(12, 4, 0)
+    forward(2)
+    pl.semaphore_wait(tok.at[0], 2)
+    token(1)
+    prepare(16, 2, 0)
+    prepare(18, 4, 1)
+    forward(3)
 
     right = lax.broadcasted_iota(jnp.int32, (8, 128), 1) >= 64
-    auxc = jnp.where(right == (core == 1), aux[...], AUXS[...])
+    auxc = jnp.where(right == (core == 1), AUX[...], AUXS[...])
     precision = auxc[0:1, :]
     class_id = ((row // 16) * 32 + core * 16 + row % 16).astype(F32)
     picks = [auxc[1:2, :] == class_id, auxc[2:3, :] == class_id]
@@ -253,60 +258,80 @@
         OH[:, k * 128 : k * 128 + 128] = jnp.where(picks[k], 1.0, 0.0).astype(BF16)
     PT[...] = jnp.zeros_like(PT)
 
-    for d in (0, 1, 2, 3):
-        got(far + (y + d) % 4, h)
+    prepare(22, 10, 1)
     own_g.wait()
-
-    low = (lax.broadcasted_iota(jnp.int32, (128, 256), 1) % 128) < 64
-    for j in range(18):
-        left = G[:, j * 128 : j * 128 + 128]
-        if j < 14:
-            tile = jnp.concatenate([left, G[:, (18 + j) * 128 : (18 + j) * 128 + 128]], axis=1)
-            keep, right_side = low, FI[j]
-        else:
-            tile, keep, right_side = left, low[:, 0:128], FI[j, 0:128, :]
-        zero = jnp.zeros_like(tile)
-        stacked = jnp.concatenate([jnp.where(keep, tile, zero), jnp.where(keep, zero, tile)], axis=0)
-        out = dot_nn(stacked, right_side)
-        even, odd = out[0:128], out[128:256]
-        k_even, k_odd = (2 * j if j <= 9 else 36 - 2 * j), (2 * j + 1 if j <= 8 else 35 - 2 * j)
-        if j <= 9:
-            F[k_even] = even[:, 0:128]
-        else:
-            F[k_even] += even[:, 0:128]
-        if 0 < k_even < 18:
+    for d in (1, 3, 2):
+        q = near_q(d)
+        arrived(G.at[rows_at(q)], agr.at[q, 0])
+
+    low = (lax.broadcasted_iota(jnp.int32, (64, 256), 1) % 128) < 64
+
+    def harmonics(first):
+        rows = pl.ds(pl.multiple_of(first * 16, 64), 64)
+        for j in range(18):
+            left = G[rows, j * 128 : j * 128 + 128]
+            if j < 14:
+                tile = jnp.concatenate([left, G[rows, (18 + j) * 128 : (18 + j) * 128 + 128]], axis=1)
+                keep, right_side = low, FI[j]
+            else:
+                tile, keep, right_side = left, low[:, 0:128], FI[j, 0:128, :]
+            zero = jnp.zeros_like(tile)
+            stacked = jnp.concatenate([jnp.where(keep, tile, zero), jnp.where(keep, zero, tile)], axis=0)
+            out = dot_nn(stacked, right_side)
+            even, odd = out[0:64], out[64:128]
+            k_even, k_odd = (2 * j if j <= 9 else 36 - 2 * j), (2 * j + 1 if j <= 8 else 35 - 2 * j)
             if j <= 9:
-                F[18 + k_even] = even[:, 128:256]
+                F[k_even, rows, :] = even[:, 0:128]
             else:
-                F[18 + k_even] += even[:, 128:256]
-        if j <= 8:
-            F[k_odd] = odd[:, 0:128]
-            F[18 + k_odd] = odd[:, 128:256]
-        else:
-            F[k_odd] += odd[:, 0:128]
-            F[18 + k_odd] += odd[:, 128:256]
-
-    square = jnp.zeros((128, 128), F32)
-    for t in range(32):
-        value = G[:, t * 128 : t * 128 + 128].astype(F32)
-        square = square + value * value
-    F[36] = jnp.broadcast_to(0.5 * jnp.sum(square, axis=1, keepdims=True), (128, 128))
+                F[k_even, rows, :] += even[:, 0:128]
+            if 0 < k_even < 18:
+                if j <= 9:
+                    F[18 + k_even, rows, :] = even[:, 128:256]
+                else:
+                    F[18 + k_even, rows, :] += even[:, 128:256]
+            if j <= 8:
+                F[k_odd, rows, :] = odd[:, 0:128]
+                F[18 + k_odd, rows, :] = odd[:, 128:256]
+            else:
+                F[k_odd, rows, :] += odd[:, 0:128]
+                F[18 + k_odd, rows, :] += odd[:, 128:256]
+        square = jnp.zeros((64, 128), F32)
+        for t in range(32):
+            value = G[rows, t * 128 : t * 128 + 128].astype(F32)
+            square = square + value * value
+        F[36, rows, :] = jnp.broadcast_to(0.5 * jnp.sum(square, axis=1, keepdims=True), (64, 128))
 
     even_row = lax.broadcasted_iota(jnp.int32, (8, 128), 0) % 2 == 0
 
-    def choose(kk, carry):
-        f = F[kk]
-        parts = []
-        for k in range(2):
-            kept = jnp.where(picks[k], f, 0.0)
-            total = tree(add, [kept[n * 8 : n * 8 + 8] for n in range(16)])
-            parts.append(total + pltpu.roll(total, 1, 0))
-        both = jnp.where(even_row, parts[0], parts[1])
-        both = both + pltpu.roll(both, 2, 0)
-        CHX[kk] = both + pltpu.roll(both, 4, 0)
-        return carry
-
-    lax.fori_loop(0, 37, choose, 0)
+    def choose(first, more):
+        rows = pl.ds(pl.multiple_of(first * 16, 64), 64)
+        ids = (((row[0:64] // 16) + first) * 32 + core * 16 + row[0:64] % 16).astype(F32)
+        keep = [auxc[k : k + 1, :] == ids for k in (1, 2)]
+
+        def step(kk, carry):
+            f = F[kk, rows, :]
+            parts = []
+            for k in range(2):
+                kept = jnp.where(keep[k], f, 0.0)
+                total = tree(add, [kept[n * 8 : n * 8 + 8] for n in range(8)])
+                parts.append(total + pltpu.roll(total, 1, 0))
+            both = jnp.where(even_row, parts[0], parts[1])
+            both = both + pltpu.roll(both, 2, 0)
+            both = both + pltpu.roll(both, 4, 0)
+            CHX[kk] = CHX[kk] + both if more else both
+            return carry
+
+        lax.fori_loop(0, 36, step, 0, unroll=4)
+        step(36, 0)
+
+    harmonics(col)
+    choose(col, False)
+    pl.semaphore_wait(tok.at[1], 2)
+    token(2)
+    for d in order:
+        arrived(piece(far_q(d), h), agr.at[far_q(d), h])
+    harmonics(far)
+    choose(far, True)
     send(CHX, CHS, sibs.at[2], sibr.at[2], sib)
     arrived(CHS, sibr.at[2])
 
@@ -356,7 +381,7 @@
                     SA[x_half, q % 4, q // 4, :, out_lanes] = block
             return carry
 
-        lax.fori_loop(0, 4, step, 0)
+        lax.fori_loop(0, 4, step, 0, unroll=True)
 
     for x_half in range(2):
         sums(x_half, 0)
@@ -373,6 +398,7 @@
         [jnp.broadcast_to(share[0:1], (8, 128)), jnp.broadcast_to(share[1:2], (8, 128))], axis=1
     )
     W0[...] = dot_nt(shares, onehot.astype(F32), precision=lax.Precision.HIGHEST)
+    pl.semaphore_wait(tok.at[2], 2)
     for d in range(1, 16):
         send(W0, RW0.at[d - 1], ws.at[d - 1], wr.at[d - 1], at_z(d))
 
@@ -461,12 +487,8 @@
 
 
 def body(images, references, precision, candidates):
-    rows = jnp.concatenate(
-        [precision.reshape(1, 64), candidates.T.astype(F32), jnp.zeros((5, 64), F32)], axis=0
-    )
-    aux = jnp.concatenate([rows, rows], axis=1)
     table = jnp.asarray(spread_table())
-    anywhere = pl.BlockSpec(memory_space=pl.ANY)
+    anywhere = pl.BlockSpec(memory_space=pltpu.HBM)
     vmem = pl.BlockSpec(memory_space=pltpu.VMEM)
     dma = pltpu.SemaphoreType.DMA
     scratch = [
@@ -475,6 +497,9 @@
         pltpu.VMEM((128, 4096), BF16),
         pltpu.VMEM((18, 256, 256), BF16),
         pltpu.VMEM((37, 128, 128), F32),
+        pltpu.VMEM((1, 64), F32),
+        pltpu.VMEM((2, 64), jnp.int32),
+        pltpu.VMEM((8, 128), F32),
         pltpu.VMEM((8, 128), F32),
         pltpu.VMEM((37, 8, 128), F32),
         pltpu.VMEM((37, 8, 128), F32),
@@ -501,8 +526,9 @@
         pltpu.VMEM((3, 8, 128), F32),
         pltpu.VMEM((16, 128), F32),
         pltpu.VMEM((16, 128), F32),
-        dma((3,)),
-        dma((14,)),
+        dma((5,)),
+        pltpu.SemaphoreType.REGULAR((3,)),
+        dma((11,)),
         dma((8, 2)),
         dma((4,)),
         dma((4,)),
@@ -518,13 +544,13 @@
     average, evidence = pl.pallas_call(
         kernel,
         out_shape=(jax.ShapeDtypeStruct((16, 128), F32), jax.ShapeDtypeStruct((1, 64), F32)),
-        in_specs=[anywhere, anywhere, vmem, anywhere],
+        in_specs=[anywhere] * 5,
         out_specs=(vmem, vmem),
         scratch_shapes=scratch,
         compiler_params=pltpu.CompilerParams(
-            collective_id=0, has_side_effects=True, vmem_limit_bytes=40 * 1024 * 1024
+            collective_id=0, has_side_effects=True, vmem_limit_bytes=60 * 1024 * 1024
         ),
-    )(images, references, aux, table)
+    )(images, references, precision.reshape(1, 64), candidates.T, table)
     return average, evidence.reshape(64)
 
 

time: 73 us -> 62 us (0.85); the launches traced: 71.9 us -> 61.8 us
  Pallas kernels: 65.1 us -> 58.7 us
  local copies, waits for them, and re-layouts: 4.65 us -> 2.43 us
  other arithmetic: 1.49 us -> 0 us
    pallas_call x1, Pallas kernels: 65.1 us -> 58.7 us  [body(): pl.pallas_call(kernel, out_shape=(jax.ShapeDtypeStruct((16, 128), F32), j...]
    unnamed x8 -> x2, local copies, waits for them, and re-layouts: 4.65 us -> 2.43 us
    concatenate x1 -> x0, other arithmetic: 0.81 us -> none  [body(): aux = jnp.concatenate([rows, rows], axis=1)]
where the time goes in v2:
time: 62 us; the launch traced here: 61.8 us
  Pallas kernels  58.7 us (95%)
  local copies, waits for them, and re-layouts  2.43 us (4%)
  between operations  0.64 us (1%)
    pallas_call x1, Pallas kernels, body(): pl.pallas_call(kernel, out_shape=(jax.ShapeDtypeStruct((16, 128), F32), j...  58.7 us
    unnamed x2, local copies, waits for them, and re-layouts  2.43 us

profile of v2, /device:TPU:1, one launch (start us, length us, event | category | flops | bytes accessed | tf_op | source)
XLA Modules:
  0.0 61.8 jit_solution(1079157790069357492)
XLA Ops:
  0.6 58.7 %shard_map.68 = (f32[16,128]{1,0:T(8,128)}, f32[1,64]{1,0:T(1,128)}) custom-call(bf16[64,4096]{1,0:T(8,128)(2,1)} %images.1, bf16[16,4096]{1,0:T(8,128)(2,1)} %refs.1, f32[1,64]{1,0:T(1,128)} %bitcast.4, s32[2,64]{1,0:T(2,128)} %bitcast.3, bf16[16,128,512]{2,1,0:T(8,128)(2,1)} %constant.2.clone.table), custom_call_target="tpu_custom_call" | custom-call | tf_op jit(solution)/shard_map/pallas_call | solution.py:544
  59.3 1.3 %copy.9 = f32[16,128]{1,0:T(8,128)} copy(f32[16,128]{1,0:T(8,128)} %get-tuple-element.8) | data formatting | bytes 16384
  60.6 1.1 %copy.10 = f32[64]{0:T(128)} copy(f32[64]{0:T(128)} %bitcast.5) | data formatting | bytes 512

commit v3 on v2

--- a/solution.py
+++ b/solution.py
@@ -139,6 +139,7 @@
         return dev(x, y, (z + d) % 16, core)
 
     sent = []
+    far_first = sorted(range(1, 16), key=lambda d: -min(d, 16 - d))
 
     def send(src, dst, ssem, rsem, to):
         copy = pltpu.make_async_remote_copy(
@@ -383,23 +384,21 @@
 
         lax.fori_loop(0, 4, step, 0, unroll=True)
 
-    for x_half in range(2):
+    other = 1 - x_lo
+    for pos, x_half in enumerate((other, x_lo)):
         sums(x_half, 0)
-        for d in range(1, 4):
-            n = x_half * 3 + d - 1
+        for d in (2, 1, 3):
+            n = pos * 3 + d - 1
             send(SA.at[x_half, (y + d) % 4], RA.at[d - 1, x_half], s1s.at[n], s1r.at[n], at_y(d))
-    for x_half in range(2):
         sums(x_half, 1)
-    for d in range(1, 4):
-        n = 5 + d
-        send(SB.at[(x + d) % 4], RB.at[d - 1], s1s.at[n], s1r.at[n], at_x(d))
-
+        for d in ((1, 3), (2,))[pos]:
+            send(SB.at[(x + d) % 4], RB.at[d - 1], s1s.at[5 + d], s1r.at[5 + d], at_x(d))
     shares = jnp.concatenate(
         [jnp.broadcast_to(share[0:1], (8, 128)), jnp.broadcast_to(share[1:2], (8, 128))], axis=1
     )
     W0[...] = dot_nt(shares, onehot.astype(F32), precision=lax.Precision.HIGHEST)
     pl.semaphore_wait(tok.at[2], 2)
-    for d in range(1, 16):
+    for d in far_first:
         send(W0, RW0.at[d - 1], ws.at[d - 1], wr.at[d - 1], at_z(d))
 
     def block_scores(n, carry):
@@ -420,15 +419,9 @@
     LS[8:16] = jnp.broadcast_to(total, (8, 128))
     send(LS, LR, sibs.at[3], sibr.at[3], sib)
 
-    for d in range(1, 16):
-        arrived(RW0.at[d - 1], wr.at[d - 1])
-    W1[...] = tree(add, [W0[...]] + [RW0[d] for d in range(15)])
-    for d in range(1, 4):
-        send(W1, RW1.at[d - 1], ws.at[14 + d], wr.at[14 + d], at_y(d))
-
-    for d in range(1, 4):
-        for x_half in range(2):
-            arrived(RA.at[d - 1, x_half], s1r.at[x_half * 3 + d - 1])
+    for pos, x_half in enumerate((other, x_lo)):
+        for d in range(1, 4):
+            arrived(RA.at[d - 1, x_half], s1r.at[pos * 3 + d - 1])
     for x_half in range(2):
         for x_top in range(2):
             total = SA[x_half, y, x_top].astype(F32)
@@ -447,18 +440,18 @@
     for d in range(1, 4):
         send(TB.at[(y + d) % 4], R2B.at[d - 1], s2s.at[2 + d], s2r.at[2 + d], at_y(d))
 
-    for d in range(1, 4):
-        arrived(RW1.at[d - 1], wr.at[14 + d])
-    W2[...] = tree(add, [W1[...]] + [RW1[d] for d in range(3)])
-    for d in range(1, 4):
-        send(W2, RW2.at[d - 1], ws.at[17 + d], wr.at[17 + d], at_x(d))
-
     arrived(LR, sibr.at[3])
     peak = jnp.maximum(LS[0:8], LR[0:8])
     total = LS[8:16] * jnp.exp(LS[0:8] - peak) + LR[8:16] * jnp.exp(LR[0:8] - peak)
     evidence = peak + jnp.log(total)
     evid_out[...] = jnp.where(core == 0, evidence[0:1, 0:64], evidence[0:1, 64:128])
 
+    for d in range(1, 16):
+        arrived(RW0.at[d - 1], wr.at[d - 1])
+    W1[...] = tree(add, [W0[...]] + [RW0[d] for d in range(15)])
+    for d in range(1, 4):
+        send(W1, RW1.at[d - 1], ws.at[14 + d], wr.at[14 + d], at_y(d))
+
     for d in range(1, 4):
         arrived(R2A.at[d - 1], s2r.at[d - 1])
     total = TA[x] + R2A[0] + R2A[1] + R2A[2]
@@ -470,8 +463,14 @@
     for n in range(8):
         UZ[8 + n] = total[:, n * 128 : n * 128 + 128]
     SZ[...] = UZ[...].astype(BF16)
-    for d in range(1, 16):
+    for d in far_first:
         send(SZ.at[(z + d) % 16], RZ.at[d - 1], zs.at[d - 1], zr.at[d - 1], at_z(d))
+
+    for d in range(1, 4):
+        arrived(RW1.at[d - 1], wr.at[14 + d])
+    W2[...] = tree(add, [W1[...]] + [RW1[d] for d in range(3)])
+    for d in range(1, 4):
+        send(W2, RW2.at[d - 1], ws.at[17 + d], wr.at[17 + d], at_x(d))
 
     for d in range(1, 4):
         arrived(RW2.at[d - 1], wr.at[17 + d])

time: 62 us -> 57.9 us (0.934)
  Pallas kernels: 58.7 us -> 54.6 us
    pallas_call x1, Pallas kernels: 58.7 us -> 54.6 us  [body(): pl.pallas_call(kernel, out_shape=(jax.ShapeDtypeStruct((16, 128), F32), j...]
where the time goes in v3:
time: 57.9 us; the launch traced here: 57.7 us
  Pallas kernels  54.6 us (94%)
  local copies, waits for them, and re-layouts  2.43 us (4%)
  between operations  0.64 us (1%)
    pallas_call x1, Pallas kernels, body(): pl.pallas_call(kernel, out_shape=(jax.ShapeDtypeStruct((16, 128), F32), j...  54.6 us
    unnamed x2, local copies, waits for them, and re-layouts  2.43 us

profile of v3, /device:TPU:1, one launch (start us, length us, event | category | flops | bytes accessed | tf_op | source)
XLA Modules:
  0.0 57.7 jit_solution(15608804495923610943)
XLA Ops:
  0.6 54.6 %shard_map.68 = (f32[16,128]{1,0:T(8,128)}, f32[1,64]{1,0:T(1,128)}) custom-call(bf16[64,4096]{1,0:T(8,128)(2,1)} %images.1, bf16[16,4096]{1,0:T(8,128)(2,1)} %refs.1, f32[1,64]{1,0:T(1,128)} %bitcast.4, s32[2,64]{1,0:T(2,128)} %bitcast.3, bf16[16,128,512]{2,1,0:T(8,128)(2,1)} %constant.2.clone.table), custom_call_target="tpu_custom_call" | custom-call | tf_op jit(solution)/shard_map/pallas_call | solution.py:543
  55.3 1.3 %copy.9 = f32[16,128]{1,0:T(8,128)} copy(f32[16,128]{1,0:T(8,128)} %get-tuple-element.8) | data formatting | bytes 16384
  56.6 1.1 %copy.10 = f32[64]{0:T(128)} copy(f32[64]{0:T(128)} %bitcast.5) | data formatting | bytes 512

commit v4 on v3

--- a/solution.py
+++ b/solution.py
@@ -127,7 +127,10 @@
 
     sib = dev(x, y, z, 1 - core)
     x_opp, x_same = 3 - x, x_hi * 2 + 1 - x_lo
-    same = dev(x_same, y, z, core)
+    zb = z % 2
+    z_pair, z_other = (z + 1 - 2 * zb) % 16, (z + 15 + 2 * zb) % 16
+    same, pair, other_z = dev(x_same, y, z, core), dev(x, y, z_pair, core), dev(x, y, z_other, core)
+    diagonal = dev(x_same, y, z_pair, core)
 
     def at_y(d):
         return dev(x, (y + d) % 4, z, core)
@@ -166,7 +169,7 @@
     barrier = pltpu.get_barrier_semaphore()
     partners = [dev(x_opp, (y + d) % 4, z, core) for d in range(1, 4)]
     partners += [at_y(d) for d in range(1, 4)] + [at_x(d) for d in range(1, 4)]
-    partners += [at_z(1), at_z(15), sib]
+    partners += [diagonal, pair, other_z, sib]
     for to in partners:
         pl.semaphore_signal(barrier, inc=1, device_id=to, device_id_type=MESH)
     own_p.wait()
@@ -183,10 +186,14 @@
     def rows_at(q):
         return pl.ds(pl.multiple_of(q * 16, 16), 16)
 
-    def piece(q, hh):
-        return G.at[rows_at(q), pl.ds(pl.multiple_of(hh * 2048, 2048), 2048)]
-
-    h = x_lo
+    def half(q, n):
+        return G.at[rows_at(q), pl.ds(pl.multiple_of(n * 2048, 2048), 2048)]
+
+    def quarter(q, n):
+        return G.at[rows_at(q), pl.ds(pl.multiple_of(n * 1024, 1024), 1024)]
+
+    mine_f, same_f = 2 * x_lo + zb, 2 * (1 - x_lo) + zb
+    pair_f, diagonal_f = 2 * x_lo + 1 - zb, 2 * (1 - x_lo) + 1 - zb
     col, far = x_hi * 4, (1 - x_hi) * 4
     order = (0, 1, 3, 2)
 
@@ -198,11 +205,13 @@
 
     send(AUX, AUXS, sibs.at[1], sibr.at[1], sib)
     send(images, IM.at[mine_rows], sibs.at[0], sibr.at[0], sib)
-    own_half = refs.at[:, pl.ds(pl.multiple_of(h * 2048, 2048), 2048)]
+    opp_quarter = refs.at[:, pl.ds(pl.multiple_of(same_f * 1024, 1024), 1024)]
+    own_half = refs.at[:, pl.ds(pl.multiple_of(zb * 2048, 2048), 2048)]
     for n, d in enumerate(order):
-        send(own_half, piece(q_me, h), ags.at[n], agr.at[q_me, h], dev(x_opp, (y + d) % 4, z, core))
+        to = dev(x_opp, (y + d) % 4, z, core)
+        send(opp_quarter, quarter(q_me, same_f), ags.at[n], agr.at[q_me, same_f], to)
     for n, d in enumerate((1, 3, 2)):
-        send(refs, G.at[rows_at(q_me)], ags.at[4 + n], agr.at[q_me, 0], at_y(d))
+        send(own_half, half(q_me, zb), ags.at[4 + n], agr.at[q_me, zb], at_y(d))
     token(0)
     own_im.wait()
     arrived(IM.at[pl.ds(pl.multiple_of((1 - core) * 64, 64), 64)], sibr.at[0])
@@ -233,22 +242,33 @@
 
         lax.fori_loop(0, count, step, 0, unroll=2)
 
-    def forward(n):
+    def hand_far(n):
         q = far_q(order[n])
-        arrived(piece(q, 1 - h), agr.at[q, 1 - h])
-        send(piece(q, 1 - h), piece(q, 1 - h), ags.at[7 + n], agr.at[q, 1 - h], same)
-
-    prepare(0, 8, 0)
-    forward(0)
-    prepare(8, 4, 0)
-    forward(1)
-    prepare(12, 4, 0)
-    forward(2)
+        part, sem = quarter(q, mine_f), agr.at[q, mine_f]
+        arrived(part, sem)
+        for m, to in enumerate((diagonal, same, pair)):
+            send(part, part, ags.at[10 + 3 * n + m], sem, to)
+
+    def hand_near(n):
+        q = near_q((1, 3, 2)[n])
+        part, sem = half(q, zb), agr.at[q, zb]
+        arrived(part, sem)
+        send(part, part, ags.at[7 + n], sem, other_z)
+
+    prepare(0, 4, 0)
+    hand_far(0)
+    prepare(4, 2, 0)
+    hand_far(1)
+    hand_far(2)
+    hand_near(0)
+    hand_near(1)
+    prepare(6, 2, 0)
+    hand_far(3)
+    hand_near(2)
     pl.semaphore_wait(tok.at[0], 2)
     token(1)
-    prepare(16, 2, 0)
-    prepare(18, 4, 1)
-    forward(3)
+    prepare(8, 10, 0)
+    prepare(18, 14, 1)
 
     right = lax.broadcasted_iota(jnp.int32, (8, 128), 1) >= 64
     auxc = jnp.where(right == (core == 1), AUX[...], AUXS[...])
@@ -259,11 +279,10 @@
         OH[:, k * 128 : k * 128 + 128] = jnp.where(picks[k], 1.0, 0.0).astype(BF16)
     PT[...] = jnp.zeros_like(PT)
 
-    prepare(22, 10, 1)
     own_g.wait()
     for d in (1, 3, 2):
         q = near_q(d)
-        arrived(G.at[rows_at(q)], agr.at[q, 0])
+        arrived(half(q, 1 - zb), agr.at[q, 1 - zb])
 
     low = (lax.broadcasted_iota(jnp.int32, (64, 256), 1) % 128) < 64
 
@@ -330,7 +349,8 @@
     pl.semaphore_wait(tok.at[1], 2)
     token(2)
     for d in order:
-        arrived(piece(far_q(d), h), agr.at[far_q(d), h])
+        for f in (same_f, pair_f, diagonal_f):
+            arrived(quarter(far_q(d), f), agr.at[far_q(d), f])
     harmonics(far)
     choose(far, True)
     send(CHX, CHS, sibs.at[2], sibr.at[2], sib)
@@ -527,8 +547,8 @@
         pltpu.VMEM((16, 128), F32),
         dma((5,)),
         pltpu.SemaphoreType.REGULAR((3,)),
-        dma((11,)),
-        dma((8, 2)),
+        dma((22,)),
+        dma((8, 4)),
         dma((4,)),
         dma((4,)),
         dma((9,)),
@@ -547,7 +567,7 @@
         out_specs=(vmem, vmem),
         scratch_shapes=scratch,
         compiler_params=pltpu.CompilerParams(
-            collective_id=0, has_side_effects=True, vmem_limit_bytes=60 * 1024 * 1024
+            collective_id=0, has_side_effects=True, vmem_limit_bytes=55200 * 1024
         ),
     )(images, references, precision.reshape(1, 64), candidates.T, table)
     return average, evidence.reshape(64)

time: 57.9 us -> 55.8 us (0.964)
  Pallas kernels: 54.6 us -> 52.6 us
    pallas_call x1, Pallas kernels: 54.6 us -> 52.6 us  [body(): pl.pallas_call(kernel, out_shape=(jax.ShapeDtypeStruct((16, 128), F32), j...]
    unnamed x2 -> x6, local copies, waits for them, and re-layouts: 2.43 us -> 2.44 us
where the time goes in v4:
time: 55.8 us; the launch traced here: 55.6 us
  Pallas kernels  52.6 us (94%)
  local copies, waits for them, and re-layouts  2.44 us (4%)
  between operations  0.65 us (1%)
    pallas_call x1, Pallas kernels, body(): pl.pallas_call(kernel, out_shape=(jax.ShapeDtypeStruct((16, 128), F32), j...  52.6 us
    unnamed x6, local copies, waits for them, and re-layouts  2.44 us

profile of v4, /device:TPU:1, one launch (start us, length us, event | category | flops | bytes accessed | tf_op | source)
XLA Modules:
  0.0 55.6 jit_solution(4883634137058391838)
XLA Ops:
  0.6 0.0 copy-start
  0.6 0.7 %copy-done = s32[64,2]{0,1:T(2,128)S(1)} copy-done((s32[64,2]{0,1:T(2,128)S(1)}, s32[64,2]{0,1:T(2,128)}, u32[]{:S(2)}) %copy-start) | copy-done | bytes 536
  1.3 0.0 copy-start.1
  1.3 0.7 %copy-done.1 = f32[64]{0:T(128)S(1)} copy-done((f32[64]{0:T(128)S(1)}, f32[64]{0:T(128)}, u32[]{:S(2)}) %copy-start.1) | copy-done | bytes 280
  2.0 52.6 %shard_map.68 = (f32[16,128]{1,0:T(8,128)S(1)}, f32[1,64]{1,0:T(1,128)S(1)}) custom-call(bf16[64,4096]{1,0:T(8,128)(2,1)} %images.1, bf16[16,4096]{1,0:T(8,128)(2,1)} %refs.1, f32[1,64]{1,0:T(1,128)S(1)} %bitcast.4, s32[2,64]{1,0:T(2,128)S(1)} %bitcast.3, bf16[16,128,512]{2,1,0:T(8,128)(2,1)} %constant.2.clone.table), custom_call_target="tpu_custom_call" | custom-call | tf_op jit(solution)/shard_map/pallas_call | solution.py:563
  54.5 0.6 %copy.9 = f32[16,128]{1,0:T(8,128)} copy(f32[16,128]{1,0:T(8,128)S(1)} %get-tuple-element.8) | data formatting | bytes 16384
  55.1 0.5 copy.10
Async XLA Ops:
  0.6 0.7 %copy-start = (s32[64,2]{0,1:T(2,128)S(1)}, s32[64,2]{0,1:T(2,128)}, u32[]{:S(2)}) copy-start(s32[64,2]{0,1:T(2,128)} %param.8) | copy-start | bytes 1540
  1.3 0.7 %copy-start.1 = (f32[64]{0:T(128)S(1)}, f32[64]{0:T(128)}, u32[]{:S(2)}) copy-start(f32[64]{0:T(128)} %param.7) | copy-start | bytes 772

commit v5 on v4

--- a/solution.py
+++ b/solution.py
@@ -19,20 +19,15 @@
 BF16 = jnp.bfloat16
 
 
-def spread_table():
-    feats = np.arange(FEATS)
-    order = feats // (2 * CYCLES)
+def factor_table():
     turns = np.arange(TURNS)
-    angle = 2.0 * math.pi / TURNS * ((turns[:, None] * order[None, :]) % TURNS)
-    out = np.zeros((16, 128, 512), np.float32)
-    for part, values in enumerate((np.cos(angle), -np.sin(angle))):
-        values = values.astype(np.float32).reshape(TURNS, 16, 256).transpose(1, 0, 2)
-        high = values.astype(ml_dtypes.bfloat16).astype(np.float32)
-        low = values - high
-        cols = slice(part * 256, part * 256 + 256)
-        out[:, 0:36, cols] = high
-        out[:, 40:76, cols] = high
-        out[:, 80:116, cols] = low
+    angle = 2.0 * math.pi / TURNS * ((np.arange(ORDERS)[:, None] * turns[None, :]) % TURNS)
+    values = np.stack([np.cos(angle), -np.sin(angle)], axis=1).reshape(2 * ORDERS, TURNS).astype(np.float32)
+    high = values.astype(ml_dtypes.bfloat16).astype(np.float32)
+    out = np.zeros((128, 128), np.float32)
+    out[:, 0:36] = high
+    out[:, 40:76] = high
+    out[:, 80:116] = values - high
     return out.astype(ml_dtypes.bfloat16)
 
 
@@ -112,7 +107,7 @@
 
 def kernel(
     images, refs, prec, cand, table, avg_out, evid_out,
-    G, IM, IMS, FI, F, PIN, CIN, AUX, AUXS, CHX, CHS, PT, PP, TE, OH, SA, RA, SB, RB, TA, R2A, TB, R2B,
+    G, IM, FI, F, PIN, CIN, AUX, AUXS, CHX, CHS, PT, H, TE, OH, SA, RA, SB, RB, TA, R2A, TB, R2B,
     UZ, SZ, RZ, W0, RW0, W1, RW1, W2, RW2, LS, LR,
     loc, tok, ags, agr, sibs, sibr, s1s, s1r, s2s, s2r, zs, zr, ws, wr,
 ):
@@ -226,7 +221,6 @@
 
     eye = jnp.where(row == lane, 1.0, 0.0)
     rows_of = jnp.concatenate([eye, swap(lane, row)], axis=0).astype(BF16)
-    cols_of = swap(row, lane).astype(BF16)
 
     def prepare(first, count, half):
         def step(n, carry):
@@ -237,7 +231,6 @@
             sign = jnp.where(j < 9, 1.0, -1.0).astype(F32)
             FI[j, half * 128 : half * 128 + 128, 0:128] = both[0:128].astype(BF16)
             FI[j, half * 128 : half * 128 + 128, 128:256] = (both[128:256] * sign).astype(BF16)
-            IMS[:, pl.ds(pl.multiple_of(t * 128, 128), 128)] = dot_nn(block, cols_of).astype(BF16)
             return carry
 
         lax.fori_loop(0, count, step, 0, unroll=2)
@@ -373,27 +366,31 @@
             PT[k, s : s + 1, :] = high[k : k + 1]
             PT[k, 40 + s : 41 + s, :] = rest[k : k + 1]
             PT[k, 80 + s : 81 + s, :] = high[k : k + 1]
+    own_t.wait()
     for k in range(2):
-        PP[k * 128 : k * 128 + 128, :] = PT[k].T.astype(BF16)
-    own_t.wait()
+        H[k] = dot_nn(TE[...], PT[k].astype(BF16))
 
     onehot = OH[...]
 
     def sums(x_half, second):
         def step(v, carry):
             u = x_half * 8 + second * 4 + v
-            lanes = pl.ds(pl.multiple_of(u * 256, 256), 256)
             out_lanes = pl.ds(pl.multiple_of(v * 256, 256), 256)
-            factor = dot_nn(PP[...], TE[u])
-            straight, turned_in = IM[:, lanes].astype(F32), IMS[:, lanes].astype(F32)
-            rows = [
-                (
-                    straight * factor[k * 128 : k * 128 + 128, 0:256]
-                    - turned_in * factor[k * 128 : k * 128 + 128, 256:512]
-                ).astype(BF16)
-                for k in range(2)
-            ]
-            out = dot_nn(onehot, jnp.concatenate(rows, axis=0)).astype(BF16)
+            upper = u // 9
+            factors = [H[k, pl.ds(pl.multiple_of(u * 8, 8), 8), :] for k in range(2)]
+            columns = [[], []]
+            for part in range(2):
+                rows = pl.ds(pl.multiple_of(upper * 128, 128), 128)
+                tile = FI[2 * u + part - 18 * upper, rows, 0:128].astype(F32)
+                for m in range(2):
+                    real, imag = tile[m * 64 : m * 64 + 32], tile[m * 64 + 32 : m * 64 + 64]
+                    for k in range(2):
+                        at = (part * 2 + m) * 2
+                        f_real, f_imag = factors[k][at : at + 1], factors[k][at + 1 : at + 2]
+                        columns[k].append((real * f_real - imag * f_imag).astype(BF16))
+                        columns[k].append((real * f_imag + imag * f_real).astype(BF16))
+            rows_in = jnp.concatenate([jnp.concatenate(c, axis=0) for c in columns], axis=1)
+            out = dot_nt(onehot, rows_in).astype(BF16)
             for q in range(8):
                 block = out[q * 16 : q * 16 + 16]
                 if second:
@@ -497,21 +494,20 @@
     weight = tree(add, [W2[...]] + [RW2[d] for d in range(3)])
     pick = lane[0:16] == row[0:16] + q_me * 16
     weight = jnp.sum(jnp.where(pick, jnp.broadcast_to(weight[0:1], (16, 128)), 0.0), axis=1, keepdims=True)
+    for copy in sent:
+        copy.wait_send()
     for d in range(1, 16):
         arrived(RZ.at[d - 1], zr.at[d - 1])
     total = tree(add, [UZ[z]] + [RZ[d].astype(F32) for d in range(15)])
     avg_out[...] = total / (1.0 + weight)
-    for copy in sent:
-        copy.wait_send()
 
 
 def body(images, references, precision, candidates):
-    table = jnp.asarray(spread_table())
+    table = jnp.asarray(factor_table())
     anywhere = pl.BlockSpec(memory_space=pltpu.HBM)
     vmem = pl.BlockSpec(memory_space=pltpu.VMEM)
     dma = pltpu.SemaphoreType.DMA
     scratch = [
-        pltpu.VMEM((128, 4096), BF16),
         pltpu.VMEM((128, 4096), BF16),
         pltpu.VMEM((128, 4096), BF16),
         pltpu.VMEM((18, 256, 256), BF16),
@@ -523,8 +519,8 @@
         pltpu.VMEM((37, 8, 128), F32),
         pltpu.VMEM((37, 8, 128), F32),
         pltpu.VMEM((2, 128, 128), F32),
-        pltpu.VMEM((256, 128), BF16),
-        pltpu.VMEM((16, 128, 512), BF16),
+        pltpu.VMEM((2, 128, 128), F32),
+        pltpu.VMEM((128, 128), BF16),
         pltpu.VMEM((128, 256), BF16),
         pltpu.VMEM((2, 4, 2, 16, 1024), BF16),
         pltpu.VMEM((3, 2, 2, 16, 1024), BF16),

time: 55.8 us -> 53.6 us (0.961)
  Pallas kernels: 52.6 us -> 51 us
  local copies, waits for them, and re-layouts: 2.44 us -> 1.78 us
    pallas_call x1, Pallas kernels: 52.6 us -> 51 us  [body(): pl.pallas_call(kernel, out_shape=(jax.ShapeDtypeStruct((16, 128), F32), j...]
    unnamed x6, local copies, waits for them, and re-layouts: 2.44 us -> 1.78 us
where the time goes in v5:
time: 53.6 us; the launch traced here: 53.5 us
  Pallas kernels  51 us (95%)
  local copies, waits for them, and re-layouts  1.78 us (3%)
  between operations  0.66 us (1%)
    pallas_call x1, Pallas kernels, body(): pl.pallas_call(kernel, out_shape=(jax.ShapeDtypeStruct((16, 128), F32), j...  51 us
    unnamed x6, local copies, waits for them, and re-layouts  1.78 us

profile of v5, /device:TPU:1, one launch (start us, length us, event | category | flops | bytes accessed | tf_op | source)
XLA Modules:
  0.0 53.5 jit_solution(8235663119171612753)
XLA Ops:
  0.6 0.0 copy-start
  0.6 0.0 copy-start.1
  0.7 0.7 %copy-done = s32[64,2]{0,1:T(2,128)S(1)} copy-done((s32[64,2]{0,1:T(2,128)S(1)}, s32[64,2]{0,1:T(2,128)}, u32[]{:S(2)}) %copy-start) | copy-done | bytes 536
  1.3 0.0 copy-done.1
  1.3 51.0 %shard_map.68 = (f32[16,128]{1,0:T(8,128)S(1)}, f32[1,64]{1,0:T(1,128)S(1)}) custom-call(bf16[64,4096]{1,0:T(8,128)(2,1)} %images.1, bf16[16,4096]{1,0:T(8,128)(2,1)} %refs.1, f32[1,64]{1,0:T(1,128)S(1)} %bitcast.4, s32[2,64]{1,0:T(2,128)S(1)} %bitcast.3, bf16[128,128]{1,0:T(8,128)(2,1)} %constant.2.clone.table), custom_call_target="tpu_custom_call" | custom-call | tf_op jit(solution)/shard_map/pallas_call | solution.py:559
  52.4 0.6 %copy.9 = f32[16,128]{1,0:T(8,128)} copy(f32[16,128]{1,0:T(8,128)S(1)} %get-tuple-element.8) | data formatting | bytes 16384
  53.0 0.5 copy.10
Async XLA Ops:
  0.6 0.7 %copy-start = (s32[64,2]{0,1:T(2,128)S(1)}, s32[64,2]{0,1:T(2,128)}, u32[]{:S(2)}) copy-start(s32[64,2]{0,1:T(2,128)} %param.8) | copy-start | bytes 1540
  0.6 0.7 %copy-start.1 = (f32[64]{0:T(128)S(1)}, f32[64]{0:T(128)}, u32[]{:S(2)}) copy-start(f32[64]{0:T(128)} %param.7) | copy-start | bytes 772

commit v6 on v5

--- a/solution.py
+++ b/solution.py
@@ -107,7 +107,7 @@
 
 def kernel(
     images, refs, prec, cand, table, avg_out, evid_out,
-    G, IM, FI, F, PIN, CIN, AUX, AUXS, CHX, CHS, PT, H, TE, OH, SA, RA, SB, RB, TA, R2A, TB, R2B,
+    G, IM, FI, F, PIN, CIN, AUX, AUXS, CHX, PS, PR, PT, H, TE, OH, SA, RA, SB, RB, TA, R2A, TB, R2B,
     UZ, SZ, RZ, W0, RW0, W1, RW1, W2, RW2, LS, LR,
     loc, tok, ags, agr, sibs, sibr, s1s, s1r, s2s, s2r, zs, zr, ws, wr,
 ):
@@ -123,9 +123,11 @@
     sib = dev(x, y, z, 1 - core)
     x_opp, x_same = 3 - x, x_hi * 2 + 1 - x_lo
     zb = z % 2
-    z_pair, z_other = (z + 1 - 2 * zb) % 16, (z + 15 + 2 * zb) % 16
-    same, pair, other_z = dev(x_same, y, z, core), dev(x, y, z_pair, core), dev(x, y, z_other, core)
-    diagonal = dev(x_same, y, z_pair, core)
+
+    def at_z_of(d):
+        return dev(x, y, (z + d) % 16, core)
+
+    same, z_up, z_dn = dev(x_same, y, z, core), at_z_of(1), at_z_of(15)
 
     def at_y(d):
         return dev(x, (y + d) % 4, z, core)
@@ -164,7 +166,7 @@
     barrier = pltpu.get_barrier_semaphore()
     partners = [dev(x_opp, (y + d) % 4, z, core) for d in range(1, 4)]
     partners += [at_y(d) for d in range(1, 4)] + [at_x(d) for d in range(1, 4)]
-    partners += [diagonal, pair, other_z, sib]
+    partners += [z_up, z_dn, sib]
     for to in partners:
         pl.semaphore_signal(barrier, inc=1, device_id=to, device_id_type=MESH)
     own_p.wait()
@@ -187,8 +189,8 @@
     def quarter(q, n):
         return G.at[rows_at(q), pl.ds(pl.multiple_of(n * 1024, 1024), 1024)]
 
-    mine_f, same_f = 2 * x_lo + zb, 2 * (1 - x_lo) + zb
-    pair_f, diagonal_f = 2 * x_lo + 1 - zb, 2 * (1 - x_lo) + 1 - zb
+    mine_f = (z + 2 * x_lo) % 4
+    same_f, up_f, dn_f = (mine_f + 2) % 4, (mine_f + 1) % 4, (mine_f + 3) % 4
     col, far = x_hi * 4, (1 - x_hi) * 4
     order = (0, 1, 3, 2)
 
@@ -206,7 +208,7 @@
         to = dev(x_opp, (y + d) % 4, z, core)
         send(opp_quarter, quarter(q_me, same_f), ags.at[n], agr.at[q_me, same_f], to)
     for n, d in enumerate((1, 3, 2)):
-        send(own_half, half(q_me, zb), ags.at[4 + n], agr.at[q_me, zb], at_y(d))
+        send(own_half, half(q_me, zb), ags.at[4 + n], agr.at[q_me, 2 * zb], at_y(d))
     token(0)
     own_im.wait()
     arrived(IM.at[pl.ds(pl.multiple_of((1 - core) * 64, 64), 64)], sibr.at[0])
@@ -239,14 +241,15 @@
         q = far_q(order[n])
         part, sem = quarter(q, mine_f), agr.at[q, mine_f]
         arrived(part, sem)
-        for m, to in enumerate((diagonal, same, pair)):
-            send(part, part, ags.at[10 + 3 * n + m], sem, to)
+        for m, to in enumerate((same, z_up, z_dn)):
+            send(part, part, ags.at[13 + 3 * n + m], sem, to)
 
     def hand_near(n):
         q = near_q((1, 3, 2)[n])
-        part, sem = half(q, zb), agr.at[q, zb]
-        arrived(part, sem)
-        send(part, part, ags.at[7 + n], sem, other_z)
+        arrived(half(q, zb), agr.at[q, 2 * zb])
+        for m, to in enumerate((z_up, z_dn)):
+            part = quarter(q, 2 * zb + m)
+            send(part, part, ags.at[7 + 2 * n + m], agr.at[q, 2 * zb + m], to)
 
     prepare(0, 4, 0)
     hand_far(0)
@@ -275,7 +278,8 @@
     own_g.wait()
     for d in (1, 3, 2):
         q = near_q(d)
-        arrived(half(q, 1 - zb), agr.at[q, 1 - zb])
+        for m in range(2):
+            arrived(quarter(q, 2 * (1 - zb) + m), agr.at[q, 2 * (1 - zb) + m])
 
     low = (lax.broadcasted_iota(jnp.int32, (64, 256), 1) % 128) < 64
 
@@ -342,33 +346,42 @@
     pl.semaphore_wait(tok.at[1], 2)
     token(2)
     for d in order:
-        for f in (same_f, pair_f, diagonal_f):
+        for f in (same_f, up_f, dn_f):
             arrived(quarter(far_q(d), f), agr.at[far_q(d), f])
     harmonics(far)
     choose(far, True)
-    send(CHX, CHS, sibs.at[2], sibr.at[2], sib)
-    arrived(CHS, sibr.at[2])
-
-    coefs = [CHX[k] + CHS[k] for k in range(37)]
+    names = jnp.where(even_row, auxc[1:2, :], auxc[2:3, :]).astype(jnp.int32)
+    held = (names // 16) % 2 == core
+
+    def both_picks(op, v):
+        return op(v, jnp.where(even_row, pltpu.roll(v, 7, 0), pltpu.roll(v, 1, 0)))
+
+    coefs = [CHX[k] for k in range(37)]
     turned = turns_of(coefs[0:19], [None] + coefs[19:36])
     scores = [precision * (v - coefs[36]) for v in turned]
-    peak = tree(jnp.maximum, scores)
-    peak = jnp.maximum(peak, jnp.where(even_row, pltpu.roll(peak, 7, 0), pltpu.roll(peak, 1, 0)))
-    exps = [jnp.exp(v - peak) for v in scores]
-    total = tree(add, exps)
-    total = total + jnp.where(even_row, pltpu.roll(total, 7, 0), pltpu.roll(total, 1, 0))
-    posterior = [v / total for v in exps]
-    share = tree(add, posterior)
+    own_peak = both_picks(jnp.maximum, jnp.where(held, tree(jnp.maximum, scores), -1e30))
+    weights = [jnp.where(held, jnp.exp(v - own_peak), 0.0) for v in scores]
+    share = tree(add, weights)
+    own_total = both_picks(add, share)
+    PS[0:8] = own_peak
+    PS[8:16] = own_total
+    send(PS, PR, sibs.at[2], sibr.at[2], sib)
     for s in range(TURNS):
-        high = posterior[s].astype(BF16).astype(F32)
-        rest = posterior[s] - high
+        high = weights[s].astype(BF16).astype(F32)
+        rest = weights[s] - high
         for k in range(2):
             PT[k, s : s + 1, :] = high[k : k + 1]
             PT[k, 40 + s : 41 + s, :] = rest[k : k + 1]
             PT[k, 80 + s : 81 + s, :] = high[k : k + 1]
     own_t.wait()
+    spectra = [dot_nn(TE[...], PT[k].astype(BF16)) for k in range(2)]
+    arrived(PR, sibr.at[2])
+    peak = jnp.maximum(own_peak, PR[0:8])
+    own_part = jnp.exp(own_peak - peak)
+    scale = own_part / (own_part * own_total + jnp.exp(PR[0:8] - peak) * PR[8:16])
+    share = share * scale
     for k in range(2):
-        H[k] = dot_nn(TE[...], PT[k].astype(BF16))
+        H[k] = spectra[k] * scale[0:1]
 
     onehot = OH[...]
 
@@ -517,7 +530,8 @@
         pltpu.VMEM((8, 128), F32),
         pltpu.VMEM((8, 128), F32),
         pltpu.VMEM((37, 8, 128), F32),
-        pltpu.VMEM((37, 8, 128), F32),
+        pltpu.VMEM((16, 128), F32),
+        pltpu.VMEM((16, 128), F32),
         pltpu.VMEM((2, 128, 128), F32),
         pltpu.VMEM((2, 128, 128), F32),
         pltpu.VMEM((128, 128), BF16),
@@ -543,7 +557,7 @@
         pltpu.VMEM((16, 128), F32),
         dma((5,)),
         pltpu.SemaphoreType.REGULAR((3,)),
-        dma((22,)),
+        dma((25,)),
         dma((8, 4)),
         dma((4,)),
         dma((4,)),

time: 53.6 us -> 53.3 us (level)
  no operation moved by 1% of the time
where the time goes in v6:
time: 53.3 us; the launch traced here: 53.1 us
  Pallas kernels  50.7 us (95%)
  local copies, waits for them, and re-layouts  1.78 us (3%)
  between operations  0.66 us (1%)
    pallas_call x1, Pallas kernels, body(): pl.pallas_call(kernel, out_shape=(jax.ShapeDtypeStruct((16, 128), F32), j...  50.7 us
    unnamed x6, local copies, waits for them, and re-layouts  1.78 us

profile of v6, /device:TPU:1, one launch (start us, length us, event | category | flops | bytes accessed | tf_op | source)
XLA Modules:
  0.0 53.1 jit_solution(14676799543139104487)
XLA Ops:
  0.6 0.0 copy-start
  0.6 0.0 copy-start.1
  0.7 0.7 %copy-done = s32[64,2]{0,1:T(2,128)S(1)} copy-done((s32[64,2]{0,1:T(2,128)S(1)}, s32[64,2]{0,1:T(2,128)}, u32[]{:S(2)}) %copy-start) | copy-done | bytes 536
  1.3 0.0 copy-done.1
  1.3 50.7 %shard_map.68 = (f32[16,128]{1,0:T(8,128)S(1)}, f32[1,64]{1,0:T(1,128)S(1)}) custom-call(bf16[64,4096]{1,0:T(8,128)(2,1)} %images.1, bf16[16,4096]{1,0:T(8,128)(2,1)} %refs.1, f32[1,64]{1,0:T(1,128)S(1)} %bitcast.4, s32[2,64]{1,0:T(2,128)S(1)} %bitcast.3, bf16[128,128]{1,0:T(8,128)(2,1)} %constant.2.clone.table), custom_call_target="tpu_custom_call" | custom-call | tf_op jit(solution)/shard_map/pallas_call | solution.py:573
  52.0 0.6 %copy.9 = f32[16,128]{1,0:T(8,128)} copy(f32[16,128]{1,0:T(8,128)S(1)} %get-tuple-element.8) | data formatting | bytes 16384
  52.6 0.5 copy.10
Async XLA Ops:
  0.6 0.7 %copy-start = (s32[64,2]{0,1:T(2,128)S(1)}, s32[64,2]{0,1:T(2,128)}, u32[]{:S(2)}) copy-start(s32[64,2]{0,1:T(2,128)} %param.8) | copy-start | bytes 1540
  0.6 0.7 %copy-start.1 = (f32[64]{0:T(128)S(1)}, f32[64]{0:T(128)}, u32[]{:S(2)}) copy-start(f32[64]{0:T(128)} %param.7) | copy-start | bytes 772

commit v7 on v6

--- a/solution.py
+++ b/solution.py
@@ -107,7 +107,7 @@
 
 def kernel(
     images, refs, prec, cand, table, avg_out, evid_out,
-    G, IM, FI, F, PIN, CIN, AUX, AUXS, CHX, PS, PR, PT, H, TE, OH, SA, RA, SB, RB, TA, R2A, TB, R2B,
+    G, IM, FI, F, PIN, CIN, AUX, AUXS, CHX, PS, PR, PT, H, TE, OH, SA, RA, SB, RB, TA, TAB, R2A, TB, TBB, R2B,
     UZ, SZ, RZ, W0, RW0, W1, RW1, W2, RW2, LS, LR,
     loc, tok, ags, agr, sibs, sibr, s1s, s1r, s2s, s2r, zs, zr, ws, wr,
 ):
@@ -458,8 +458,9 @@
             for d in range(3):
                 total = total + RA[d, x_half, x_top].astype(F32)
             TA[x_top * 2 + x_half] = total
-    for d in range(1, 4):
-        send(TA.at[(x + d) % 4], R2A.at[d - 1], s2s.at[d - 1], s2r.at[d - 1], at_x(d))
+            TAB[x_top * 2 + x_half] = total.astype(BF16)
+    for d in range(1, 4):
+        send(TAB.at[(x + d) % 4], R2A.at[d - 1], s2s.at[d - 1], s2r.at[d - 1], at_x(d))
     for d in range(1, 4):
         arrived(RB.at[d - 1], s1r.at[5 + d])
     for y_to in range(4):
@@ -467,8 +468,9 @@
         for d in range(3):
             total = total + RB[d, y_to].astype(F32)
         TB[y_to] = total
-    for d in range(1, 4):
-        send(TB.at[(y + d) % 4], R2B.at[d - 1], s2s.at[2 + d], s2r.at[2 + d], at_y(d))
+        TBB[y_to] = total.astype(BF16)
+    for d in range(1, 4):
+        send(TBB.at[(y + d) % 4], R2B.at[d - 1], s2s.at[2 + d], s2r.at[2 + d], at_y(d))
 
     arrived(LR, sibr.at[3])
     peak = jnp.maximum(LS[0:8], LR[0:8])
@@ -484,12 +486,12 @@
 
     for d in range(1, 4):
         arrived(R2A.at[d - 1], s2r.at[d - 1])
-    total = TA[x] + R2A[0] + R2A[1] + R2A[2]
+    total = TA[x] + R2A[0].astype(F32) + R2A[1].astype(F32) + R2A[2].astype(F32)
     for n in range(8):
         UZ[n] = total[:, n * 128 : n * 128 + 128]
     for d in range(1, 4):
         arrived(R2B.at[d - 1], s2r.at[2 + d])
-    total = TB[y] + R2B[0] + R2B[1] + R2B[2]
+    total = TB[y] + R2B[0].astype(F32) + R2B[1].astype(F32) + R2B[2].astype(F32)
     for n in range(8):
         UZ[8 + n] = total[:, n * 128 : n * 128 + 128]
     SZ[...] = UZ[...].astype(BF16)
@@ -541,9 +543,11 @@
         pltpu.VMEM((4, 4, 16, 1024), BF16),
         pltpu.VMEM((3, 4, 16, 1024), BF16),
         pltpu.VMEM((4, 16, 1024), F32),
-        pltpu.VMEM((3, 16, 1024), F32),
+        pltpu.VMEM((4, 16, 1024), BF16),
+        pltpu.VMEM((3, 16, 1024), BF16),
         pltpu.VMEM((4, 16, 1024), F32),
-        pltpu.VMEM((3, 16, 1024), F32),
+        pltpu.VMEM((4, 16, 1024), BF16),
+        pltpu.VMEM((3, 16, 1024), BF16),
         pltpu.VMEM((16, 16, 128), F32),
         pltpu.VMEM((16, 16, 128), BF16),
         pltpu.VMEM((15, 16, 128), BF16),

time: 53.3 us -> 51.3 us (0.962)
  Pallas kernels: 50.7 us -> 48.8 us
    pallas_call x1, Pallas kernels: 50.7 us -> 48.8 us  [body(): pl.pallas_call(kernel, out_shape=(jax.ShapeDtypeStruct((16, 128), F32), j...]
where the time goes in v7:
time: 51.3 us; the launch traced here: 51.2 us
  Pallas kernels  48.8 us (95%)
  local copies, waits for them, and re-layouts  1.78 us (3%)
  between operations  0.66 us (1%)
    pallas_call x1, Pallas kernels, body(): pl.pallas_call(kernel, out_shape=(jax.ShapeDtypeStruct((16, 128), F32), j...  48.8 us
    unnamed x6, local copies, waits for them, and re-layouts  1.78 us

profile of v7, /device:TPU:1, one launch (start us, length us, event | category | flops | bytes accessed | tf_op | source)
XLA Modules:
  0.0 51.2 jit_solution(17790407228862012444)
XLA Ops:
  0.6 0.0 copy-start
  0.6 0.0 copy-start.1
  0.7 0.7 %copy-done = s32[64,2]{0,1:T(2,128)S(1)} copy-done((s32[64,2]{0,1:T(2,128)S(1)}, s32[64,2]{0,1:T(2,128)}, u32[]{:S(2)}) %copy-start) | copy-done | bytes 536
  1.3 0.0 copy-done.1
  1.3 48.8 %shard_map.68 = (f32[16,128]{1,0:T(8,128)S(1)}, f32[1,64]{1,0:T(1,128)S(1)}) custom-call(bf16[64,4096]{1,0:T(8,128)(2,1)} %images.1, bf16[16,4096]{1,0:T(8,128)(2,1)} %refs.1, f32[1,64]{1,0:T(1,128)S(1)} %bitcast.4, s32[2,64]{1,0:T(2,128)S(1)} %bitcast.3, bf16[128,128]{1,0:T(8,128)(2,1)} %constant.2.clone.table), custom_call_target="tpu_custom_call" | custom-call | tf_op jit(solution)/shard_map/pallas_call | solution.py:577
  50.1 0.6 %copy.9 = f32[16,128]{1,0:T(8,128)} copy(f32[16,128]{1,0:T(8,128)S(1)} %get-tuple-element.8) | data formatting | bytes 16384
  50.7 0.5 copy.10
Async XLA Ops:
  0.6 0.7 %copy-start = (s32[64,2]{0,1:T(2,128)S(1)}, s32[64,2]{0,1:T(2,128)}, u32[]{:S(2)}) copy-start(s32[64,2]{0,1:T(2,128)} %param.8) | copy-start | bytes 1540
  0.6 0.7 %copy-start.1 = (f32[64]{0:T(128)S(1)}, f32[64]{0:T(128)}, u32[]{:S(2)}) copy-start(f32[64]{0:T(128)} %param.7) | copy-start | bytes 772

commit v8 on v6

--- a/solution.py
+++ b/solution.py
@@ -107,8 +107,8 @@
 
 def kernel(
     images, refs, prec, cand, table, avg_out, evid_out,
-    G, IM, FI, F, PIN, CIN, AUX, AUXS, CHX, PS, PR, PT, H, TE, OH, SA, RA, SB, RB, TA, R2A, TB, R2B,
-    UZ, SZ, RZ, W0, RW0, W1, RW1, W2, RW2, LS, LR,
+    G, IM, FI, F, PIN, CIN, AUX, AUXS, CHX, PS, PR, PT, H, TE, OH, SA, RA, SB, RB, TA, TAB, R2A, TB, TBB, R2B,
+    OA, OB, UZ, SZ, RZ, W0, RW0, W1, RW1, W2, RW2, LS, LR,
     loc, tok, ags, agr, sibs, sibr, s1s, s1r, s2s, s2r, zs, zr, ws, wr,
 ):
     img, blk = lax.axis_index("img"), lax.axis_index("blk")
@@ -385,7 +385,7 @@
 
     onehot = OH[...]
 
-    def sums(x_half, second):
+    def sums(x_half, second, mine):
         def step(v, carry):
             u = x_half * 8 + second * 4 + v
             out_lanes = pl.ds(pl.multiple_of(v * 256, 256), 256)
@@ -403,7 +403,17 @@
                         columns[k].append((real * f_real - imag * f_imag).astype(BF16))
                         columns[k].append((real * f_imag + imag * f_real).astype(BF16))
             rows_in = jnp.concatenate([jnp.concatenate(c, axis=0) for c in columns], axis=1)
-            out = dot_nt(onehot, rows_in).astype(BF16)
+            exact = dot_nt(onehot, rows_in)
+            out = exact.astype(BF16)
+            parts = [exact[q * 16 : q * 16 + 16] for q in range(8)]
+            if second and mine:
+                for n in range(4):
+                    OB[n, :, out_lanes] = jnp.where(x_hi == 0, parts[n], parts[4 + n])
+            if not second:
+                for n in range(2):
+                    four = parts[n * 4 : n * 4 + 4]
+                    lower, upper_two = jnp.where(y == 0, four[0], four[1]), jnp.where(y == 2, four[2], four[3])
+                    OA[n * 2 + x_half, :, out_lanes] = jnp.where(y < 2, lower, upper_two)
             for q in range(8):
                 block = out[q * 16 : q * 16 + 16]
                 if second:
@@ -415,14 +425,14 @@
         lax.fori_loop(0, 4, step, 0, unroll=True)
 
     other = 1 - x_lo
-    for pos, x_half in enumerate((other, x_lo)):
-        sums(x_half, 0)
+    for pos, x_half in enumerate((x_lo, other)):
+        sums(x_half, 1, pos == 0)
+        for d in ((2,), (1, 3))[pos]:
+            send(SB.at[(x + d) % 4], RB.at[d - 1], s1s.at[5 + d], s1r.at[5 + d], at_x(d))
+        sums(x_half, 0, pos == 0)
         for d in (2, 1, 3):
-            n = pos * 3 + d - 1
+            n = (1 - pos) * 3 + d - 1
             send(SA.at[x_half, (y + d) % 4], RA.at[d - 1, x_half], s1s.at[n], s1r.at[n], at_y(d))
-        sums(x_half, 1)
-        for d in ((1, 3), (2,))[pos]:
-            send(SB.at[(x + d) % 4], RB.at[d - 1], s1s.at[5 + d], s1r.at[5 + d], at_x(d))
     shares = jnp.concatenate(
         [jnp.broadcast_to(share[0:1], (8, 128)), jnp.broadcast_to(share[1:2], (8, 128))], axis=1
     )
@@ -452,23 +462,28 @@
     for pos, x_half in enumerate((other, x_lo)):
         for d in range(1, 4):
             arrived(RA.at[d - 1, x_half], s1r.at[pos * 3 + d - 1])
-    for x_half in range(2):
-        for x_top in range(2):
-            total = SA[x_half, y, x_top].astype(F32)
-            for d in range(3):
-                total = total + RA[d, x_half, x_top].astype(F32)
-            TA[x_top * 2 + x_half] = total
-    for d in range(1, 4):
-        send(TA.at[(x + d) % 4], R2A.at[d - 1], s2s.at[d - 1], s2r.at[d - 1], at_x(d))
+    for d in (2, 1, 3, 0):
+        x_to = (x + d) % 4
+        total = OA[x_to]
+        for n in range(3):
+            total = total + RA[n, x_to % 2, x_to // 2].astype(F32)
+        if d:
+            TAB[d - 1] = total.astype(BF16)
+            send(TAB.at[d - 1], R2A.at[d - 1], s2s.at[d - 1], s2r.at[d - 1], at_x(d))
+        else:
+            TA[...] = total
     for d in range(1, 4):
         arrived(RB.at[d - 1], s1r.at[5 + d])
-    for y_to in range(4):
-        total = SB[x, y_to].astype(F32)
-        for d in range(3):
-            total = total + RB[d, y_to].astype(F32)
-        TB[y_to] = total
-    for d in range(1, 4):
-        send(TB.at[(y + d) % 4], R2B.at[d - 1], s2s.at[2 + d], s2r.at[2 + d], at_y(d))
+    for d in (2, 1, 3, 0):
+        y_to = (y + d) % 4
+        total = OB[y_to]
+        for n in range(3):
+            total = total + RB[n, y_to].astype(F32)
+        if d:
+            TBB[d - 1] = total.astype(BF16)
+            send(TBB.at[d - 1], R2B.at[d - 1], s2s.at[2 + d], s2r.at[2 + d], at_y(d))
+        else:
+            TB[...] = total
 
     arrived(LR, sibr.at[3])
     peak = jnp.maximum(LS[0:8], LR[0:8])
@@ -484,12 +499,12 @@
 
     for d in range(1, 4):
         arrived(R2A.at[d - 1], s2r.at[d - 1])
-    total = TA[x] + R2A[0] + R2A[1] + R2A[2]
+    total = TA[...] + R2A[0].astype(F32) + R2A[1].astype(F32) + R2A[2].astype(F32)
     for n in range(8):
         UZ[n] = total[:, n * 128 : n * 128 + 128]
     for d in range(1, 4):
         arrived(R2B.at[d - 1], s2r.at[2 + d])
-    total = TB[y] + R2B[0] + R2B[1] + R2B[2]
+    total = TB[...] + R2B[0].astype(F32) + R2B[1].astype(F32) + R2B[2].astype(F32)
     for n in range(8):
         UZ[8 + n] = total[:, n * 128 : n * 128 + 128]
     SZ[...] = UZ[...].astype(BF16)
@@ -540,10 +555,14 @@
         pltpu.VMEM((3, 2, 2, 16, 1024), BF16),
         pltpu.VMEM((4, 4, 16, 1024), BF16),
         pltpu.VMEM((3, 4, 16, 1024), BF16),
+        pltpu.VMEM((16, 1024), F32),
+        pltpu.VMEM((3, 16, 1024), BF16),
+        pltpu.VMEM((3, 16, 1024), BF16),
+        pltpu.VMEM((16, 1024), F32),
+        pltpu.VMEM((3, 16, 1024), BF16),
+        pltpu.VMEM((3, 16, 1024), BF16),
         pltpu.VMEM((4, 16, 1024), F32),
-        pltpu.VMEM((3, 16, 1024), F32),
         pltpu.VMEM((4, 16, 1024), F32),
-        pltpu.VMEM((3, 16, 1024), F32),
         pltpu.VMEM((16, 16, 128), F32),
         pltpu.VMEM((16, 16, 128), BF16),
         pltpu.VMEM((15, 16, 128), BF16),

time: 53.3 us -> 50.9 us (0.955)
  Pallas kernels: 50.7 us -> 48.4 us
    pallas_call x1, Pallas kernels: 50.7 us -> 48.4 us  [body(): pl.pallas_call(kernel, out_shape=(jax.ShapeDtypeStruct((16, 128), F32), j...]
where the time goes in v8:
time: 50.9 us; the launch traced here: 50.8 us
  Pallas kernels  48.4 us (95%)
  local copies, waits for them, and re-layouts  1.78 us (3%)
  between operations  0.66 us (1%)
    pallas_call x1, Pallas kernels, body(): pl.pallas_call(kernel, out_shape=(jax.ShapeDtypeStruct((16, 128), F32), j...  48.4 us
    unnamed x6, local copies, waits for them, and re-layouts  1.78 us

profile of v8, /device:TPU:1, one launch (start us, length us, event | category | flops | bytes accessed | tf_op | source)
XLA Modules:
  0.0 50.8 jit_solution(7938057029432630818)
XLA Ops:
  0.6 0.0 copy-start
  0.6 0.0 copy-start.1
  0.7 0.7 %copy-done = s32[64,2]{0,1:T(2,128)S(1)} copy-done((s32[64,2]{0,1:T(2,128)S(1)}, s32[64,2]{0,1:T(2,128)}, u32[]{:S(2)}) %copy-start) | copy-done | bytes 536
  1.3 0.0 copy-done.1
  1.3 48.4 %shard_map.68 = (f32[16,128]{1,0:T(8,128)S(1)}, f32[1,64]{1,0:T(1,128)S(1)}) custom-call(bf16[64,4096]{1,0:T(8,128)(2,1)} %images.1, bf16[16,4096]{1,0:T(8,128)(2,1)} %refs.1, f32[1,64]{1,0:T(1,128)S(1)} %bitcast.4, s32[2,64]{1,0:T(2,128)S(1)} %bitcast.3, bf16[128,128]{1,0:T(8,128)(2,1)} %constant.2.clone.table), custom_call_target="tpu_custom_call" | custom-call | tf_op jit(solution)/shard_map/pallas_call | solution.py:592
  49.7 0.6 %copy.9 = f32[16,128]{1,0:T(8,128)} copy(f32[16,128]{1,0:T(8,128)S(1)} %get-tuple-element.8) | data formatting | bytes 16384
  50.3 0.5 %copy.10 = f32[64]{0:T(128)} copy(f32[64]{0:T(128)S(1)} %bitcast.5) | data formatting | bytes 512
Async XLA Ops:
  0.6 0.7 %copy-start = (s32[64,2]{0,1:T(2,128)S(1)}, s32[64,2]{0,1:T(2,128)}, u32[]{:S(2)}) copy-start(s32[64,2]{0,1:T(2,128)} %param.8) | copy-start | bytes 1540
  0.6 0.7 %copy-start.1 = (f32[64]{0:T(128)S(1)}, f32[64]{0:T(128)}, u32[]{:S(2)}) copy-start(f32[64]{0:T(128)} %param.7) | copy-start | bytes 772

commit v9 on v8

--- a/solution.py
+++ b/solution.py
@@ -122,8 +122,6 @@
 
     sib = dev(x, y, z, 1 - core)
     x_opp, x_same = 3 - x, x_hi * 2 + 1 - x_lo
-    zb = z % 2
-
     def at_z_of(d):
         return dev(x, y, (z + d) % 16, core)
 
@@ -183,9 +181,6 @@
     def rows_at(q):
         return pl.ds(pl.multiple_of(q * 16, 16), 16)
 
-    def half(q, n):
-        return G.at[rows_at(q), pl.ds(pl.multiple_of(n * 2048, 2048), 2048)]
-
     def quarter(q, n):
         return G.at[rows_at(q), pl.ds(pl.multiple_of(n * 1024, 1024), 1024)]
 
@@ -203,12 +198,11 @@
     send(AUX, AUXS, sibs.at[1], sibr.at[1], sib)
     send(images, IM.at[mine_rows], sibs.at[0], sibr.at[0], sib)
     opp_quarter = refs.at[:, pl.ds(pl.multiple_of(same_f * 1024, 1024), 1024)]
-    own_half = refs.at[:, pl.ds(pl.multiple_of(zb * 2048, 2048), 2048)]
     for n, d in enumerate(order):
         to = dev(x_opp, (y + d) % 4, z, core)
         send(opp_quarter, quarter(q_me, same_f), ags.at[n], agr.at[q_me, same_f], to)
     for n, d in enumerate((1, 3, 2)):
-        send(own_half, half(q_me, zb), ags.at[4 + n], agr.at[q_me, 2 * zb], at_y(d))
+        send(refs, G.at[rows_at(q_me)], ags.at[4 + n], agr.at[q_me, 0], at_y(d))
     token(0)
     own_im.wait()
     arrived(IM.at[pl.ds(pl.multiple_of((1 - core) * 64, 64), 64)], sibr.at[0])
@@ -244,23 +238,13 @@
         for m, to in enumerate((same, z_up, z_dn)):
             send(part, part, ags.at[13 + 3 * n + m], sem, to)
 
-    def hand_near(n):
-        q = near_q((1, 3, 2)[n])
-        arrived(half(q, zb), agr.at[q, 2 * zb])
-        for m, to in enumerate((z_up, z_dn)):
-            part = quarter(q, 2 * zb + m)
-            send(part, part, ags.at[7 + 2 * n + m], agr.at[q, 2 * zb + m], to)
-
     prepare(0, 4, 0)
     hand_far(0)
     prepare(4, 2, 0)
     hand_far(1)
     hand_far(2)
-    hand_near(0)
-    hand_near(1)
     prepare(6, 2, 0)
     hand_far(3)
-    hand_near(2)
     pl.semaphore_wait(tok.at[0], 2)
     token(1)
     prepare(8, 10, 0)
@@ -278,8 +262,7 @@
     own_g.wait()
     for d in (1, 3, 2):
         q = near_q(d)
-        for m in range(2):
-            arrived(quarter(q, 2 * (1 - zb) + m), agr.at[q, 2 * (1 - zb) + m])
+        arrived(G.at[rows_at(q)], agr.at[q, 0])
 
     low = (lax.broadcasted_iota(jnp.int32, (64, 256), 1) % 128) < 64
 

time: 50.9 us -> 49.9 us (0.980)
  Pallas kernels: 48.4 us -> 47.3 us
    pallas_call x1, Pallas kernels: 48.4 us -> 47.3 us  [body(): pl.pallas_call(kernel, out_shape=(jax.ShapeDtypeStruct((16, 128), F32), j...]
where the time goes in v9:
time: 49.9 us; the launch traced here: 49.8 us
  Pallas kernels  47.3 us (95%)
  local copies, waits for them, and re-layouts  1.78 us (4%)
  between operations  0.66 us (1%)
    pallas_call x1, Pallas kernels, body(): pl.pallas_call(kernel, out_shape=(jax.ShapeDtypeStruct((16, 128), F32), j...  47.3 us
    unnamed x6, local copies, waits for them, and re-layouts  1.78 us

profile of v9, /device:TPU:1, one launch (start us, length us, event | category | flops | bytes accessed | tf_op | source)
XLA Modules:
  0.0 49.8 jit_solution(4255274312539627090)
XLA Ops:
  0.6 0.0 copy-start
  0.6 0.0 copy-start.1
  0.7 0.7 %copy-done = s32[64,2]{0,1:T(2,128)S(1)} copy-done((s32[64,2]{0,1:T(2,128)S(1)}, s32[64,2]{0,1:T(2,128)}, u32[]{:S(2)}) %copy-start) | copy-done | bytes 536
  1.3 0.0 copy-done.1
  1.3 47.3 %shard_map.68 = (f32[16,128]{1,0:T(8,128)S(1)}, f32[1,64]{1,0:T(1,128)S(1)}) custom-call(bf16[64,4096]{1,0:T(8,128)(2,1)} %images.1, bf16[16,4096]{1,0:T(8,128)(2,1)} %refs.1, f32[1,64]{1,0:T(1,128)S(1)} %bitcast.4, s32[2,64]{1,0:T(2,128)S(1)} %bitcast.3, bf16[128,128]{1,0:T(8,128)(2,1)} %constant.2.clone.table), custom_call_target="tpu_custom_call" | custom-call | tf_op jit(solution)/shard_map/pallas_call | solution.py:575
  48.7 0.6 %copy.9 = f32[16,128]{1,0:T(8,128)} copy(f32[16,128]{1,0:T(8,128)S(1)} %get-tuple-element.8) | data formatting | bytes 16384
  49.3 0.5 %copy.10 = f32[64]{0:T(128)} copy(f32[64]{0:T(128)S(1)} %bitcast.5) | data formatting | bytes 512
Async XLA Ops:
  0.6 0.7 %copy-start = (s32[64,2]{0,1:T(2,128)S(1)}, s32[64,2]{0,1:T(2,128)}, u32[]{:S(2)}) copy-start(s32[64,2]{0,1:T(2,128)} %param.8) | copy-start | bytes 1540
  0.6 0.7 %copy-start.1 = (f32[64]{0:T(128)S(1)}, f32[64]{0:T(128)}, u32[]{:S(2)}) copy-start(f32[64]{0:T(128)} %param.7) | copy-start | bytes 772

commit v10 on v9

--- a/solution.py
+++ b/solution.py
@@ -196,13 +196,13 @@
         return far + (y + d) % 4
 
     send(AUX, AUXS, sibs.at[1], sibr.at[1], sib)
-    send(images, IM.at[mine_rows], sibs.at[0], sibr.at[0], sib)
     opp_quarter = refs.at[:, pl.ds(pl.multiple_of(same_f * 1024, 1024), 1024)]
     for n, d in enumerate(order):
         to = dev(x_opp, (y + d) % 4, z, core)
         send(opp_quarter, quarter(q_me, same_f), ags.at[n], agr.at[q_me, same_f], to)
     for n, d in enumerate((1, 3, 2)):
         send(refs, G.at[rows_at(q_me)], ags.at[4 + n], agr.at[q_me, 0], at_y(d))
+    send(images, IM.at[mine_rows], sibs.at[0], sibr.at[0], sib)
     token(0)
     own_im.wait()
     arrived(IM.at[pl.ds(pl.multiple_of((1 - core) * 64, 64), 64)], sibr.at[0])

time: 49.9 us -> 49.9 us (level)
  no operation moved by 1% of the time
where the time goes in v10:
time: 49.9 us; the launch traced here: 49.7 us
  Pallas kernels  47.2 us (95%)
  local copies, waits for them, and re-layouts  1.78 us (4%)
  between operations  0.66 us (1%)
    pallas_call x1, Pallas kernels, body(): pl.pallas_call(kernel, out_shape=(jax.ShapeDtypeStruct((16, 128), F32), j...  47.2 us
    unnamed x6, local copies, waits for them, and re-layouts  1.78 us

profile of v10, /device:TPU:1, one launch (start us, length us, event | category | flops | bytes accessed | tf_op | source)
XLA Modules:
  0.0 49.7 jit_solution(11619450982643599522)
XLA Ops:
  0.6 0.0 copy-start
  0.6 0.0 copy-start.1
  0.7 0.7 %copy-done = s32[64,2]{0,1:T(2,128)S(1)} copy-done((s32[64,2]{0,1:T(2,128)S(1)}, s32[64,2]{0,1:T(2,128)}, u32[]{:S(2)}) %copy-start) | copy-done | bytes 536
  1.3 0.0 copy-done.1
  1.3 47.2 %shard_map.68 = (f32[16,128]{1,0:T(8,128)S(1)}, f32[1,64]{1,0:T(1,128)S(1)}) custom-call(bf16[64,4096]{1,0:T(8,128)(2,1)} %images.1, bf16[16,4096]{1,0:T(8,128)(2,1)} %refs.1, f32[1,64]{1,0:T(1,128)S(1)} %bitcast.4, s32[2,64]{1,0:T(2,128)S(1)} %bitcast.3, bf16[128,128]{1,0:T(8,128)(2,1)} %constant.2.clone.table), custom_call_target="tpu_custom_call" | custom-call | tf_op jit(solution)/shard_map/pallas_call | solution.py:575
  48.6 0.6 %copy.9 = f32[16,128]{1,0:T(8,128)} copy(f32[16,128]{1,0:T(8,128)S(1)} %get-tuple-element.8) | data formatting | bytes 16384
  49.2 0.5 %copy.10 = f32[64]{0:T(128)} copy(f32[64]{0:T(128)S(1)} %bitcast.5) | data formatting | bytes 512
Async XLA Ops:
  0.6 0.7 %copy-start = (s32[64,2]{0,1:T(2,128)S(1)}, s32[64,2]{0,1:T(2,128)}, u32[]{:S(2)}) copy-start(s32[64,2]{0,1:T(2,128)} %param.8) | copy-start | bytes 1540
  0.6 0.7 %copy-start.1 = (f32[64]{0:T(128)S(1)}, f32[64]{0:T(128)}, u32[]{:S(2)}) copy-start(f32[64]{0:T(128)} %param.7) | copy-start | bytes 772
